TPU v7x, 256 devices: a whole 4x4x8 slice. The times are simulated.
256 devices in a mesh: pool: 32 (over z, x), head: 8 (over y, core).
Axes of the slice: x: 4, y: 4, z: 8, core: 2. Of those that a mesh axis runs over, the one named last changes fastest.
Arguments:
- query: bfloat16 [8, 8192], P(None, 'head'), may hold values from -240 to 240, as said below
- query_pos: int32 [8], replicated, may hold values from 65536 to 69631
- key_latent: bfloat16 [8, 65536, 160], P(None, 'pool'), may hold values from -12 to 12
- key_up: bfloat16 [160, 1024], P(None, 'head'), may hold values from -0.5 to 0.5
- value_cache: bfloat16 [65536, 8, 1024], P('pool', None, 'head'), may hold values from -48 to 48
- chosen: int32 [8, 1024], replicated, may hold values from 0 to 8191, as said below
- value_slot: int32 [65536], replicated, may hold values from 0 to 65535, as said below
- out_weight: bfloat16 [8192, 8192], P('head', 'pool'), may hold values from -0.0625 to 0.0625
Outputs:
- mixed_out: bfloat16 [8, 8192], P(None, ('pool', 'head'))
Inputs may be any that keep to these rules, and one draw needn't show every extreme that they name: `query`: entries of the shown draw lie within -6 to 6; in general a row of one head may be scaled by up to 40. `chosen`: each row lists 1024 distinct blocks of one sequence. Block c has its latents on pool index c // 256. Of one row, at most 64 blocks fall on one pool index; in every draw one pool index receives exactly 64 blocks of every row. `value_slot`: A permutation of the storage slots; slot v lies on pool index v // 2048. Among all chosen blocks, at most 16 have their value slot on one pool index and their latents on one other (or the same) pool index; in every draw some latent-holding pool index gets exactly 16 from every storing pool index.
All inputs are finite; a program needn't handle non-finite values.
Results may differ from a plain program's by a relative error of at most 0.035.
Values may be sent and summed in bfloat16 or wider, within the bound.
No kernel may reach another device: no remote copies, remote signals or barrier semaphores. Data moves between devices by JAX's collectives and lax.ppermute only.
A program may use at most 128 MiB of HBM per device.

v0:
```python
import math

import jax
import jax.numpy as jnp
from jax import lax
from jax.sharding import PartitionSpec as P

H = 64
KVH = 8
HD = 128
RANK = 160
SPAN = 8
MOST = 64


theta_base = 500000.0


def rotate(values, positions):
    half_width = values.shape[-1] // 2
    freq_index = jnp.arange(half_width, dtype=jnp.float32)
    inverse_freq = jnp.exp(-(2.0 * freq_index / values.shape[-1]) * math.log(theta_base))
    angles = positions.astype(jnp.float32)[..., None] * inverse_freq
    cosine = jnp.cos(angles)
    sine_part = jnp.sin(angles)
    first_half = values[..., :half_width]
    second = values[..., half_width:]
    return jnp.concatenate(
        [first_half * cosine - second * sine_part, second * cosine + first_half * sine_part],
        axis=-1,
    )


def group_ranks(member, group_ids, group_total):
    entry_total = group_ids.shape[0]
    block_rows = math.gcd(entry_total, 128)
    onehot = (
        (group_ids[:, None] == jnp.arange(group_total, dtype=jnp.int32)[None, :]) & member[:, None]
    ).astype(jnp.float32)
    blocks = onehot.reshape(entry_total // block_rows, block_rows, group_total)
    lower = (
        jnp.arange(block_rows, dtype=jnp.int32)[:, None]
        >= jnp.arange(block_rows, dtype=jnp.int32)[None, :]
    ).astype(jnp.float32)
    inner = jnp.einsum("ij,bjg->big", lower, blocks, precision=lax.Precision.HIGHEST)
    block_total = inner[:, -1, :]
    offsets = jnp.cumsum(block_total, axis=0) - block_total
    running = (inner + offsets[:, None, :]).reshape(entry_total, group_total)
    return (jnp.sum(onehot * running, axis=1) - 1.0).astype(jnp.int32)


def compact_rows(row_ids, facts, row_total):
    match_table = (jnp.arange(row_total, dtype=jnp.int32)[:, None] == row_ids[None, :]).astype(
        jnp.float32
    )
    picked = jnp.dot(match_table, facts, precision=lax.Precision.HIGHEST)
    live_rows = jnp.sum(match_table, axis=1) > 0.5
    return (picked, live_rows)


def on_device(query, query_pos, key_latent, key_up, value_cache, chosen, value_slot, out_weight):
    my_pool = lax.axis_index("pool")
    pool_count = lax.axis_size("pool")
    seq_count = query.shape[0]
    width_kv = key_up.shape[1]
    kv_local = width_kv // HD
    group_size = H // KVH
    local_heads = kv_local * group_size
    per_holder = key_latent.shape[1] // SPAN
    slot_count = value_cache.shape[0]
    context_spans = per_holder * pool_count
    capacity = seq_count * MOST // pool_count
    buffer_rows = pool_count * capacity
    score_scale = 1.0 / math.sqrt(HD)
    seq_flat = jnp.broadcast_to(
        jnp.arange(seq_count, dtype=jnp.int32)[:, None], chosen.shape
    ).reshape(-1)
    chosen_flat = chosen.reshape(-1)
    slot_of = value_slot[seq_flat * context_spans + chosen_flat]
    owner_of = slot_of // slot_count
    holder_of = chosen_flat // per_holder
    seq_float = seq_flat.astype(jnp.float32)
    is_held = holder_of == my_pool
    held_rank = group_ranks(is_held, owner_of, pool_count)
    held_row = jnp.where(is_held, owner_of * capacity + held_rank, -1)
    held_facts = jnp.stack(
        [(chosen_flat - my_pool * per_holder).astype(jnp.float32), seq_float], axis=1
    )
    held_info, held_live = compact_rows(held_row, held_facts, buffer_rows)
    held_span = jnp.where(held_live, held_info[:, 0], 0.0).astype(jnp.int32)
    held_seq = jnp.where(held_live, held_info[:, 1], 0.0).astype(jnp.int32)
    is_owned = owner_of == my_pool
    owned_rank = group_ranks(is_owned, holder_of, pool_count)
    owned_row = jnp.where(is_owned, holder_of * capacity + owned_rank, -1)
    owned_facts = jnp.stack(
        [(slot_of - my_pool * slot_count).astype(jnp.float32), seq_float], axis=1
    )
    owned_info, owned_live = compact_rows(owned_row, owned_facts, buffer_rows)
    send_slot = jnp.where(owned_live, owned_info[:, 0], 0.0).astype(jnp.int32)
    latent_blocks = key_latent.reshape(seq_count, per_holder, SPAN * RANK)
    picked_blocks = latent_blocks[held_seq, held_span]
    rebuilt = jnp.dot(
        picked_blocks.reshape(buffer_rows * SPAN, RANK), key_up, preferred_element_type=jnp.float32
    )
    rebuilt = rebuilt.reshape(buffer_rows * SPAN, kv_local, HD)
    key_pos = (
        (my_pool * per_holder + held_span)[:, None] * SPAN
        + jnp.arange(SPAN, dtype=jnp.int32)[None, :]
    ).reshape(-1)
    key_rows = rotate(rebuilt, key_pos[:, None]).astype(jnp.bfloat16)
    queries = rotate(
        query.astype(jnp.float32).reshape(seq_count, kv_local, group_size, HD),
        query_pos[:, None, None],
    ).astype(jnp.bfloat16)
    block_scores = (
        jnp.einsum("skgd,nkd->skgn", queries, key_rows, preferred_element_type=jnp.float32)
        * score_scale
    )
    token_seq = jnp.repeat(jnp.where(held_live, held_seq, -1), SPAN)
    valid = (token_seq[None, :] == jnp.arange(seq_count, dtype=jnp.int32)[:, None])[
        :, None, None, :
    ]
    masked = jnp.where(valid, block_scores, -jnp.inf)
    local_peak = jnp.max(masked, axis=-1)
    global_peak = lax.pmax(local_peak, "pool")
    weights = jnp.where(valid, jnp.exp(masked - global_peak[..., None]), 0.0).astype(jnp.bfloat16)
    totals = jnp.sum(weights.astype(jnp.float32), axis=-1)
    outgoing = value_cache[send_slot].reshape(pool_count, capacity, SPAN, width_kv)
    arrived = lax.all_to_all(outgoing, "pool", split_axis=0, concat_axis=0, tiled=True)
    arrived = arrived.reshape(buffer_rows * SPAN, kv_local, HD)
    partial_value = jnp.einsum(
        "skgn,nkd->skgd", weights, arrived, preferred_element_type=jnp.float32
    )
    partial_sum, total_sum = (
        lax.psum(
            partial_value.reshape(seq_count, local_heads * HD).astype(jnp.bfloat16), "pool"
        ).astype(jnp.float32),
        lax.psum(totals.reshape(seq_count, local_heads).astype(jnp.bfloat16), "pool").astype(
            jnp.float32
        ),
    )
    attended = (
        (partial_sum.reshape(seq_count, local_heads, HD) / total_sum[..., None])
        .reshape(seq_count, local_heads * HD)
        .astype(jnp.bfloat16)
    )
    projected = jnp.dot(attended, out_weight, preferred_element_type=jnp.float32)
    return lax.psum_scatter(projected, "head", scatter_dimension=1, tiled=True).astype(jnp.bfloat16)


def solution(mesh):
    placed = (
        P(None, "head"),
        P(),
        P(None, "pool", None),
        P(None, "head"),
        P("pool", None, "head"),
        P(),
        P(),
        P("head", "pool"),
    )
    return jax.shard_map(
        on_device, mesh=mesh, in_specs=placed, out_specs=P(None, ("pool", "head")), check_vma=False
    )
```

profile of v0, /device:TPU:1, one launch (start us, length us, event | category | flops | bytes accessed | tf_op | source)
XLA Modules:
  0.0 414.3 jit_solution(6052013004950541811)
XLA Ops:
  6.5 0.0 copy-start
  6.6 0.8 reshape.586
  7.4 0.8 convert_bitcast_fusion.1
  8.3 45.5 %gather_fusion = s32[8192]{0:T(1024)S(1)} fusion(s32[65536]{0:T(1024)S(1)} %copy-done.1, s32[8192]{0:T(1024)S(1)} %broadcast_clamp_fusion), kind=kCustom, calls=%fused_computation | custom fusion | bytes 98304 | tf_op jit(solution)/shard_map/gather | solution.py:79
  53.8 0.1 broadcast_compare_fusion
  53.9 0.1 copy.92
  54.0 0.1 copy.93
  54.1 0.5 fusion.6
  54.6 1.8 copy.94
  56.5 1.3 fusion.28
  57.8 3.0 copy.95
  60.8 0.1 copy.96
  60.9 0.1 fusion.62
  61.0 0.1 copy.97
  61.1 1.1 select_reduce_fusion.1
  62.2 0.1 copy.98
  62.2 0.1 copy.99
  62.4 0.1 copy.100
  62.5 0.5 fusion.7
  63.0 1.8 copy.101
  64.8 1.3 fusion.26
  66.1 3.0 copy.102
  69.2 0.0 copy-start.2
  69.2 0.1 copy.103
  69.3 0.1 fusion.63
  69.3 0.1 copy.104
  69.4 1.1 select_reduce_fusion
  70.5 0.1 copy.105
  70.6 0.1 copy.115
  70.7 0.0 copy-done.2
  70.7 0.1 fusion.39
  70.7 2.6 convert_reduce_fusion.1
  73.4 7.5 %compare_select_fusion.3 = s32[512,1]{0,1:T(1,128)S(1)} fusion(pred[512,1]{0,1:T(4,128)(4,1)S(1)} %gt.29, f32[8192,1]{0,1:T(1,128)S(1)} %bitcast.152, f32[8192,1]{0,1:T(1,128)S(1)} %bitcast.151, s32[8192]{0:T(1024)S(1)} %get-tuple-element.13), kind=kOutput, calls=%fused_computation.117 | convolution fusion | flops 54536704 | bytes 100864 | tf_op jit(solution)/shard_map/dot_general | solution.py:56
  80.8 0.0 copy-start.4
  80.9 0.0 copy-start.5
  80.9 4.2 %gather_fusion.1 = bf16[512,8,128]{2,1,0:T(8,128)(2,1)} fusion(bf16[2048,8,128]{2,1,0:T(8,128)(2,1)} %param.12, s32[1024]{0:T(1024)S(1)} %pad_clamp_fusion), kind=kCustom, calls=%fused_computation.1 | custom fusion | bytes 2099200 | tf_op jit(solution)/shard_map/gather | solution.py:128
  85.1 12.0 %all-to-all-start = ((bf16[32,16,8,128]{3,2,1,0:T(8,128)(2,1)}), bf16[32,16,8,128]{3,2,1,0:T(8,128)(2,1)}, u32[]{:S(2)}, u32[]{:S(2)}) async-start(bf16[32,16,8,128]{3,2,1,0:T(8,128)(2,1)} %bitcast.8), calls=%async_computation | async-start | bytes 2097152 | tf_op jit(solution)/shard_map/all_to_all | solution.py:129
  97.1 0.0 reduce-scatter.4.cloned.1.call-start
  97.2 10.6 %copy.106 = bf16[8,2048,160]{2,1,0:T(8,128)(2,1)} copy(bf16[8,2048,160]{1,2,0:T(8,128)(2,1)} %param.10) | data formatting | bytes 10485760 | tf_op args[2]
  107.9 14.2 %reshape.589 = bf16[8,256,1280]{2,1,0:T(8,128)(2,1)} reshape(bf16[8,2048,160]{2,1,0:T(8,128)(2,1)} %copy.106) | data formatting | bytes 10485760 | tf_op jit(solution)/shard_map/reshape | solution.py:100
  122.1 2.4 convert_reduce_fusion
  124.5 7.4 %fusion = f32[512,2]{0,1:T(2,128)S(1)} fusion(s32[8192]{0:T(1024)S(1)} %get-tuple-element.14, f32[8192,1]{0,1:T(1,128)S(1)} %bitcast.153, f32[8192,1]{0,1:T(1,128)S(1)} %bitcast.154), kind=kOutput, calls=%fused_computation.5 | convolution fusion | flops 104873984 | bytes 102400 | tf_op jit(solution)/shard_map/dot_general | solution.py:56
  132.1 16.9 %gather_fusion.2 = bf16[512,1280]{1,0:T(8,128)(2,1)} fusion(bf16[8,256,1280]{2,1,0:T(8,128)(2,1)} %reshape.589, s32[512]{0:T(512)S(1)} %bitcast.141), kind=kCustom, calls=%fused_computation.2 | custom fusion | bytes 2625536 | tf_op jit(solution)/shard_map/gather | solution.py:101
  148.9 3.9 reshape.590
  152.9 0.1 add_convert_fusion
  153.0 0.1 convert_element_type.159
  153.2 0.1 broadcast_in_dim.42
  153.3 0.2 eq.125
  153.5 0.1 multiply_cosine_fusion.1
  153.6 0.8 convolution_bitcast_fusion
  154.4 0.1 fusion.46
  154.5 4.4 %fusion.23 = (bf16[4096,64]{0,1:T(8,128)(2,1)S(1)}, bf16[4096,64]{0,1:T(8,128)(2,1)S(1)}) fusion(f32[4096,1,128]{0,2,1:T(8,128)S(1)} %convolution_bitcast_fusion, f32[64]{0:T(128)S(1)} %multiply_exponential_fusion, f32[4096]{0:T(1024)S(1)} %convert_element_type.159), kind=kLoop, calls=%fused_computation.42 | loop fusion | flops 2359296 | bytes 3162368 | tf_op jit(solution)/shard_map/concatenate | solution.py:28
  159.0 0.5 fusion.61
  159.5 60.1 %pmax.7 = f32[8,8]{1,0:T(8,128)S(1)} all-reduce(f32[8,8]{1,0:T(8,128)S(1)} %get-tuple-element.24), channel_id=1, replica_groups=mesh['pool'=32,'head'=8] {'pool'}, use_global_device_ids=true, to_apply=%region_7.8 | all-reduce | flops 64 | bytes 512 | tf_op jit(solution)/shard_map/pmax | solution.py:125
  219.6 0.4 fusion.30
  220.0 0.0 all-to-all-done
  220.0 1.6 fusion.12
  221.6 110.3 %all-reduce = (bf16[8,8]{1,0:T(8,128)(2,1)S(1)}, bf16[8,1024]{1,0:T(8,128)(2,1)S(1)}) all-reduce(bf16[8,8]{1,0:T(8,128)(2,1)S(1)} %fusion.30, bf16[8,1024]{1,0:T(8,128)(2,1)S(1)} %bitcast.150), channel_id=1, replica_groups=mesh['pool'=32,'head'=8] {'pool'}, use_global_device_ids=true, to_apply=%region_10.11 | all-reduce | flops 8256 | bytes 33024 | tf_op jit(solution)/shard_map/psum | solution.py:138
  331.9 0.1 copy.108
  332.0 0.0 copy-done
  332.0 1.0 convolution_bitcast_fusion.1
  333.0 0.0 reduce-scatter.4.cloned.1.call-update
  333.1 73.0 %reduce-scatter.4.cloned.1.call-done = f32[32,8]{1,0:T(8,128)} async-done(((f32[256,8]{1,0:T(8,128)}), f32[32,8]{1,0:T(8,128)}) %reduce-scatter.4.cloned.1.call-update) | async-done | bytes 1040
  406.1 1.4 copy.112
  (30 shorter events, 0.4 us)
Async XLA Ops:
  6.5 325.5 %copy-start = (bf16[1024,256]{1,0:T(8,128)(2,1)S(1)}, bf16[1024,256]{1,0:T(8,128)(2,1)}, u32[]{:S(2)}) copy-start(bf16[1024,256]{1,0:T(8,128)(2,1)} %param.15) | copy-start | bytes 1572868
  6.5 1.7 copy-start.1
  69.2 1.5 copy-start.2
  80.8 16.3 %copy-start.4 = (bf16[8,1024]{1,0:T(8,128)(2,1)S(1)}, bf16[8,1024]{1,0:T(8,128)(2,1)}, u32[]{:S(2)}) copy-start(bf16[8,1024]{1,0:T(8,128)(2,1)} %param.8) | copy-start | bytes 49156
  80.9 16.4 %copy-start.5 = (s32[8]{0:T(128)S(1)}, s32[8]{0:T(128)}, u32[]{:S(2)}) copy-start(s32[8]{0:T(128)} %param.9) | copy-start | bytes 100
  85.1 134.9 %all-to-all-start = ((bf16[32,16,8,128]{3,2,1,0:T(8,128)(2,1)}), bf16[32,16,8,128]{3,2,1,0:T(8,128)(2,1)}, u32[]{:S(2)}, u32[]{:S(2)}) async-start(bf16[32,16,8,128]{3,2,1,0:T(8,128)(2,1)} %bitcast.8), calls=%async_computation | async-start | bytes 2097152 | tf_op jit(solution)/shard_map/all_to_all | solution.py:129
  97.1 308.9 %reduce-scatter.4.cloned.1.call-start = ((), (), s32[]{:S(2)}) async-start(), calls=%async_computation.2 | async-start | bytes 147456
  148.9 4.6 %copy-start.3 = (bf16[160,128]{1,0:T(8,128)(2,1)S(1)}, bf16[160,128]{1,0:T(8,128)(2,1)}, u32[]{:S(2)}) copy-start(bf16[160,128]{1,0:T(8,128)(2,1)} %param.11) | copy-start | bytes 122884
Sparse Core Ops, SparseCore 0:
  333.2 72.8 reduce-scatter.3
where the time goes:
time: 417 us; the launch traced here: 414 us
  blocking collectives  170 us (41%)
  local copies, waits for them, and re-layouts  109 us (26%)
  waiting for transfers between devices  73 us (18%)
  matrix products  21.5 us (5%)
  other arithmetic  14.6 us (4%)
  between operations  13.8 us (3%)
  starting transfers between devices  12 us (3%)
    psum x1, blocking collectives, on_device(): lax.psum(totals.reshape(seq_count, local_heads).astype(jnp.bfloat16), 'po...  110 us
    unnamed x2, waiting for transfers between devices  73 us
    pmax x1, blocking collectives, on_device(): global_peak = lax.pmax(local_peak, 'pool')  60.1 us
    gather x1, local copies, waits for them, and re-layouts, on_device(): slot_of = value_slot[seq_flat * context_spans + chosen_flat]  45.5 us
    gather x1, local copies, waits for them, and re-layouts, on_device(): picked_blocks = latent_blocks[held_seq, held_span]  16.9 us
    dot_general x2, matrix products, compact_rows(): picked = jnp.dot(match_table, facts, precision=lax.Precision.HIGHEST)  14.9 us
    reshape x1, local copies, waits for them, and re-layouts, on_device(): latent_blocks = key_latent.reshape(seq_count, per_holder, SPAN * RANK)  14.2 us
    unnamed x19, local copies, waits for them, and re-layouts  12.2 us
  transfers between devices with their start and end apart: 2, of which 1 were waited for; matrix products, arithmetic and copies ran while one was open for 15% of the time, Pallas kernels for 0%

commit v1 on v0

v1 whole, which is shorter than its diff:
```python
import math

import jax
import jax.numpy as jnp
import numpy as np
from jax import lax
from jax.experimental import pallas as pl
from jax.experimental.pallas import tpu as pltpu
from jax.sharding import PartitionSpec as P

SEQS = 8
HEADS = 8
HD = 128
HALF = HD // 2
RANK = 160
SPAN = 8
THETA = 500000.0
LANES = 128

POOLS = 32
CAP = 16
ROWS = POOLS * CAP
SPANS = 256
TOKENS = SPANS * SPAN
SLOTS = 2048
CHUNKS = SEQS * SPANS // LANES
BIG_NEG = -1e30

f32 = jnp.float32
bf16 = jnp.bfloat16

HI_ROWS, MID_ROWS, LO_ROWS = 40, 16, 128
MID_AT, LO_AT = HI_ROWS, HI_ROWS + MID_ROWS


def angle_tables():
    inverse = np.exp(-(2.0 * np.arange(HALF) / HD) * math.log(THETA))
    rows = np.concatenate([np.arange(HI_ROWS) * 2048.0, np.arange(MID_ROWS) * 128.0, np.arange(LO_ROWS) * 1.0])
    angles = rows[:, None] * inverse[None, :]
    row_table = np.concatenate([np.cos(angles), np.sin(angles)], axis=1).astype(np.float32)
    lanes = np.arange(LANES)
    columns = np.concatenate([np.minimum(lanes, HI_ROWS - 1) * 2048.0, np.minimum(lanes, MID_ROWS - 1) * 128.0, lanes * 1.0])
    angles = inverse[:, None] * columns[None, :]
    column_table = np.concatenate([np.cos(angles), np.sin(angles)], axis=0).astype(np.float32)
    return row_table, column_table


def iota(shape, dim):
    return lax.broadcasted_iota(jnp.int32, shape, dim)


def onehot(condition):
    return jnp.where(condition, 1.0, 0.0).astype(bf16)


def dot(a, b):
    return lax.dot_general(a, b, (((1,), (0,)), ((), ())), preferred_element_type=f32)


def dot_nt(a, b):
    return lax.dot_general(a, b, (((1,), (1,)), ((), ())), preferred_element_type=f32)


def pieces_of(x):
    first = x.astype(bf16).astype(f32)
    rest = x - first
    second = rest.astype(bf16).astype(f32)
    return first, second, rest - second


def rotate_queries(pos_ref, query_ref, row_ref, angle_scr, q_scr, q_out):
    for s in range(SEQS):
        pos = pos_ref[s]
        angle_scr[0, s : s + 1, :] = row_ref[pl.ds(pos >> 11, 1), :]
        angle_scr[1, s : s + 1, :] = row_ref[pl.ds(MID_AT + ((pos >> 7) & 15), 1), :]
        angle_scr[2, s : s + 1, :] = row_ref[pl.ds(LO_AT + (pos & 127), 1), :]
    first, second, third = angle_scr[0], angle_scr[1], angle_scr[2]
    cosine = first[:, :HALF] * second[:, :HALF] - first[:, HALF:] * second[:, HALF:]
    sine = first[:, HALF:] * second[:, :HALF] + first[:, :HALF] * second[:, HALF:]
    cosine, sine = (
        cosine * third[:, :HALF] - sine * third[:, HALF:],
        sine * third[:, :HALF] + cosine * third[:, HALF:],
    )
    for h in range(HEADS):
        rows = query_ref[:, h * HD : (h + 1) * HD].astype(f32)
        a, b = rows[:, :HALF], rows[:, HALF:]
        turned = jnp.concatenate([a * cosine - b * sine, b * cosine + a * sine], axis=1)
        q_scr[h * SEQS : (h + 1) * SEQS, :] = turned.astype(bf16).astype(f32)
    for s in range(SEQS):
        q_out[s] = q_scr[pl.ds(s, HEADS, stride=SEQS), :]


def key_angles(pool, column_ref, cos_scr, sin_scr):
    lane = iota((HD, LANES), 1)
    base = jnp.sum(jnp.where(lane == pool, column_ref[:, :LANES], 0.0), axis=1, keepdims=True)
    cp, sp = base[:HALF], base[HALF:]
    c2, s2 = column_ref[:HALF, LANES : 2 * LANES], column_ref[HALF:, LANES : 2 * LANES]
    cb, sb = cp * c2 - sp * s2, sp * c2 + cp * s2
    c3, s3 = column_ref[:HALF, 2 * LANES :], column_ref[HALF:, 2 * LANES :]
    for c in range(TOKENS // LANES):
        ca, sa = cb[:, c : c + 1], sb[:, c : c + 1]
        cos_scr[:, c * LANES : (c + 1) * LANES] = ca * c3 - sa * s3
        sin_scr[:, c * LANES : (c + 1) * LANES] = sa * c3 + ca * s3


def plan(pool, chosen_ref, slot_ref, slot_scr, span_scr, seq_scr, meta_scr):
    relative = chosen_ref[...] - pool * SPANS
    here = (relative >= 0) & (relative < SPANS)
    row_code = jnp.where(here, 2 * iota(relative.shape, 0) + (relative >> 7), -1)
    lane_code = relative & 127
    picks = relative.shape[1]
    member = jnp.zeros((CHUNKS, LANES), f32)
    for s in range(SEQS):
        left = onehot(iota((CHUNKS, picks), 0) == row_code[s : s + 1, :])
        right = onehot(iota((LANES, picks), 0) == lane_code[s : s + 1, :])
        member = member + dot_nt(left, right)
    for s in range(SEQS):
        slot_scr[2 * s : 2 * s + 2, :] = slot_ref[pl.ds(s * (SPANS * POOLS // LANES) + 2 * pool, 2), :]
    slots = slot_scr[...]
    owner = jnp.where(member > 0.5, slots >> 11, -1)
    local_slot = slots & (SLOTS - 1)
    owners = [jnp.where(iota((POOLS, LANES), 0) == owner[c : c + 1, :], 1.0, 0.0) for c in range(CHUNKS)]
    earlier = iota((LANES, 2 * LANES), 0) < iota((LANES, 2 * LANES), 1)
    counted = dot(jnp.concatenate(owners, axis=0).astype(bf16), onehot(earlier))
    carry = jnp.zeros((POOLS, LANES), f32)
    facts = []
    for c in range(CHUNKS):
        part = counted[c * POOLS : (c + 1) * POOLS]
        rank = jnp.sum(owners[c] * (part[:, :LANES] + carry), axis=0, keepdims=True).astype(jnp.int32)
        carry = carry + part[:, LANES:]
        at_rank = jnp.where(iota((CAP, LANES), 0) == rank, 1.0, 0.0)
        span = (iota((1, LANES), 1) + (c % 2) * LANES).astype(f32)
        slot = local_slot[c : c + 1, :]
        facts.append(
            jnp.concatenate(
                [
                    at_rank * span,
                    at_rank * float(c // 2 + 1),
                    at_rank * (slot >> 6).astype(f32),
                    at_rank * (slot & 63).astype(f32),
                ],
                axis=0,
            )
        )
    table = dot_nt(
        jnp.concatenate(owners, axis=1).astype(bf16), jnp.concatenate(facts, axis=1).astype(bf16)
    )
    spread = dot(onehot((iota((ROWS, POOLS), 0) >> 4) == iota((ROWS, POOLS), 1)), table.astype(bf16))
    own = (iota(spread.shape, 1) & (CAP - 1)) == (iota(spread.shape, 0) & (CAP - 1))
    kind = iota((4 * CAP, 3 * LANES), 0) >> 4
    column = iota((4 * CAP, 3 * LANES), 1)
    fold = onehot(
        ((column < LANES) & (kind == 0))
        | ((column >= LANES) & (column < 2 * LANES) & (kind == 1))
        | ((column == 2 * LANES + 88) & (kind == 2))
        | ((column == 2 * LANES + 89) & (kind == 3))
        | ((column == 2 * LANES + 90) & (kind == 1))
    )
    known = dot(jnp.where(own, spread, 0.0).astype(bf16), fold)
    span_scr[...] = known[:, :LANES]
    seq_scr[...] = known[:, LANES : 2 * LANES]
    meta_scr[...] = known[:, 2 * LANES :]


def pack_rows(score_scr, turned_scr, span_scr, seq_scr, meta_scr, out_ref):
    scores = score_scr[...]
    first = scores.astype(bf16).astype(f32)
    turned_scr[...] = jnp.concatenate([first, scores - first], axis=0).T
    parts = [turned_scr[pl.ds(t, SPANS, stride=SPAN), :].astype(bf16) for t in range(SPAN)]
    by_span = jnp.concatenate(parts, axis=1)
    width = SPAN * LANES
    source = iota((width, LANES), 0)
    target = iota((width, LANES), 1)
    fold = onehot(((source >> 7) == ((target & 63) >> 3)) & ((source & 7) == (target & 7)))
    block = 128
    lane = iota((block, LANES), 1)
    lane_seq = ((lane & 63) >> 3).astype(f32) + 1.0
    for start in range(0, ROWS, block):
        span = span_scr[start : start + block, :]
        seq = seq_scr[start : start + block, :]
        pick = jnp.concatenate([onehot(lane.astype(f32) == span), onehot((lane + LANES).astype(f32) == span)], axis=1)
        found = dot(pick, by_span)
        mine = seq == lane_seq
        kept = [jnp.where(mine, found[:, t * LANES : (t + 1) * LANES], 0.0) for t in range(SPAN)]
        score = dot(jnp.concatenate(kept, axis=1).astype(bf16), fold) * (1.0 / math.sqrt(HD))
        peak = score
        for shift in (8, 16, 32):
            peak = jnp.maximum(peak, pltpu.roll(peak, shift, 1))
        weight = jnp.where(seq > 0.5, jnp.exp(score - peak), 0.0)
        one, two, three = pieces_of(peak)
        packed = jnp.where(lane < 88, three, meta_scr[start : start + block, :])
        packed = jnp.where(lane < 80, two, packed)
        packed = jnp.where(lane < 72, one, packed)
        packed = jnp.where(lane < 64, weight, packed)
        out_ref[start : start + block, :] = packed.astype(bf16)


def holder_kernel(
    pos_hbm, query_hbm, latent_hbm, key_up_hbm, chosen_hbm, slot_hbm, row_hbm, column_hbm, out_ref,
    pos_ref, query_ref, latent_ref, key_up_ref, chosen_ref, slot_ref, row_ref, column_ref, sems,
    angle_scr, q_scr, q_out, up_scr, cos_scr, sin_scr, slot_scr, span_scr, seq_scr, meta_scr, score_scr, turned_scr,
):
    small = [
        pltpu.make_async_copy(source, target, sems.at[i])
        for i, (source, target) in enumerate(
            [
                (chosen_hbm, chosen_ref),
                (slot_hbm, slot_ref),
                (pos_hbm, pos_ref),
                (row_hbm, row_ref),
                (column_hbm, column_ref),
                (query_hbm, query_ref),
                (key_up_hbm, key_up_ref),
            ]
        )
    ]
    for copy in small:
        copy.start()
    latents = [pltpu.make_async_copy(latent_hbm.at[s], latent_ref.at[s], sems.at[len(small) + s]) for s in range(SEQS)]
    for copy in latents:
        copy.start()
    for copy in small:
        copy.wait()
    pool = lax.axis_index("pool")
    plan(pool, chosen_ref, slot_ref, slot_scr, span_scr, seq_scr, meta_scr)
    rotate_queries(pos_ref, query_ref, row_ref, angle_scr, q_scr, q_out)
    key_angles(pool, column_ref, cos_scr, sin_scr)
    up_scr[...] = key_up_ref[...].astype(f32).T.astype(bf16)
    score_all(latents, latent_ref, up_scr, q_out, cos_scr, sin_scr, score_scr)
    pack_rows(score_scr, turned_scr, span_scr, seq_scr, meta_scr, out_ref)


def score_all(latents, latent_ref, up_scr, q_out, cos_scr, sin_scr, score_scr):
    up = up_scr[...]
    cosine, sine = cos_scr[...], sin_scr[...]
    for s in range(SEQS):
        latents[s].wait()
        keys = dot(up, latent_ref[s])
        a, b = keys[:HALF], keys[HALF:]
        turned = jnp.concatenate([a * cosine - b * sine, b * cosine + a * sine], axis=0).astype(bf16)
        score_scr[s * HEADS : (s + 1) * HEADS, :] = dot(q_out[s].astype(bf16), turned)


def owner_kernel(
    packed_ref, values_ref, out_ref, slot_vec, slot_sca, sem, found_scr, sum_scr, level_scr
):
    packed = packed_ref[...].astype(f32).T
    slot_vec[...] = (packed[88:89] * 64.0 + packed[89:90]).astype(jnp.int32)
    copy = pltpu.make_async_copy(slot_vec, slot_sca, sem)
    copy.start()
    seq = packed[90:91]
    live = seq > 0.5
    peak = jnp.where(live, packed[64:72] + packed[72:80] + packed[80:88], BIG_NEG)
    mine = [seq == float(s + 1) for s in range(SEQS)]
    tops = [jnp.max(jnp.where(mine[s], peak, BIG_NEG), axis=1, keepdims=True) for s in range(SEQS)]
    top = jnp.zeros_like(peak)
    for s in range(SEQS):
        top = jnp.where(mine[s], tops[s], top)
    factor = jnp.where(live, jnp.exp(peak - top), 0.0)
    weights = [(packed[t * HEADS : (t + 1) * HEADS] * factor).astype(bf16).astype(f32) for t in range(SPAN)]
    over_span = weights[0]
    for t in range(1, SPAN):
        over_span = over_span + weights[t]
    totals = jnp.concatenate(
        [jnp.sum(jnp.where(mine[s], over_span, 0.0), axis=1, keepdims=True) for s in range(SEQS)], axis=0
    )
    peaks = jnp.concatenate(tops, axis=0)
    copy.wait()

    @pl.loop(0, ROWS // 16)
    def _(step):
        for i in range(16):
            row = step * 16 + i
            found_scr[pl.ds(pl.multiple_of(row * SPAN, SPAN), SPAN), :] = values_ref[slot_sca[0, row]].astype(f32)

    summed = jnp.zeros((SEQS * HEADS, HD), f32)
    for t in range(SPAN):
        left = jnp.concatenate([jnp.where(mine[s], weights[t], 0.0) for s in range(SEQS)], axis=0).astype(bf16)
        right = found_scr[pl.ds(t, ROWS, stride=SPAN), :].astype(bf16)
        summed = summed + dot(left, right)
    some = totals > 0.0
    safe = jnp.where(some, totals, 1.0)
    sum_scr[...] = summed / safe
    level = jnp.where(some, peaks + jnp.log(safe), BIG_NEG)
    level_scr[...] = jnp.broadcast_to(level, level_scr.shape)
    lane = iota((SEQS, LANES), 1)
    tail = jnp.zeros((SEQS, LANES), f32)
    parts = []
    for h in range(HEADS):
        parts.append(sum_scr[pl.ds(h, SEQS, stride=HEADS), :])
        tail = jnp.where((lane & 7) == h, level_scr[pl.ds(h, SEQS, stride=HEADS), :], tail)
    one, two, three = pieces_of(tail)
    parts.append(jnp.where(lane < 8, one, jnp.where(lane < 16, two, jnp.where(lane < 24, three, 0.0))))
    result = jnp.concatenate(parts, axis=1).astype(bf16)
    for p in range(POOLS):
        out_ref[p] = result


def combine_kernel(gathered_ref, weight_ref, out_ref):
    levels = []
    for p in range(POOLS):
        tail = gathered_ref[p, :, HEADS * HD :].astype(f32)
        levels.append(tail + pltpu.roll(tail, LANES - 8, 1) + pltpu.roll(tail, LANES - 16, 1))
    top = levels[0]
    for p in range(1, POOLS):
        top = jnp.maximum(top, levels[p])
    shares = [jnp.exp(level - top) for level in levels]
    total = shares[0]
    for p in range(1, POOLS):
        total = total + shares[p]
    inverse = 1.0 / total
    sums = [jnp.zeros((SEQS, HD), f32) for _ in range(HEADS)]
    for p in range(POOLS):
        share = shares[p] * inverse
        for h in range(HEADS):
            sums[h] = sums[h] + share[:, h : h + 1] * gathered_ref[p, :, h * HD : (h + 1) * HD].astype(f32)
    attended = jnp.concatenate(sums, axis=1).astype(bf16)
    projected = dot(attended, weight_ref[...])
    groups = out_ref.shape[0]
    width = projected.shape[1] // groups
    for g in range(groups):
        at = g * width
        half = projected[:, at // LANES * LANES : (at // LANES + 1) * LANES]
        out_ref[g] = pltpu.roll(half, (LANES - at % LANES) % LANES, 1)


def finish_kernel(parts_ref, out_ref):
    total = parts_ref[0]
    for g in range(1, parts_ref.shape[0]):
        total = total + parts_ref[g]
    out_ref[...] = total[:, : out_ref.shape[1]].astype(bf16)


def score(*operands):
    buffers = [pltpu.SMEM(operands[0].shape, jnp.int32)]
    buffers += [pltpu.VMEM(x.shape, x.dtype) for x in operands[1:]]
    return pl.pallas_call(
        holder_kernel,
        in_specs=[pl.BlockSpec(memory_space=pltpu.HBM)] * len(operands),
        out_specs=pl.BlockSpec(memory_space=pltpu.VMEM),
        out_shape=jax.ShapeDtypeStruct((ROWS, LANES), bf16),
        scratch_shapes=[
            *buffers,
            pltpu.SemaphoreType.DMA((len(operands) - 1 + SEQS,)),
            pltpu.VMEM((3, SEQS, LANES), f32),
            pltpu.VMEM((SEQS * HEADS, HD), f32),
            pltpu.VMEM((SEQS, HEADS, HD), f32),
            pltpu.VMEM((HD, RANK), bf16),
            pltpu.VMEM((HALF, TOKENS), f32),
            pltpu.VMEM((HALF, TOKENS), f32),
            pltpu.VMEM((CHUNKS, LANES), jnp.int32),
            pltpu.VMEM((ROWS, LANES), f32),
            pltpu.VMEM((ROWS, LANES), f32),
            pltpu.VMEM((ROWS, LANES), f32),
            pltpu.VMEM((SEQS * HEADS, TOKENS), f32),
            pltpu.VMEM((TOKENS, LANES), f32),
        ],
        compiler_params=pltpu.CompilerParams(vmem_limit_bytes=63_400_000),
        name="score",
    )(*operands)


def weigh(packed, values):
    return pl.pallas_call(
        owner_kernel,
        in_specs=[pl.BlockSpec(memory_space=pltpu.VMEM)] * 2,
        out_specs=pl.BlockSpec(memory_space=pltpu.VMEM),
        out_shape=jax.ShapeDtypeStruct((POOLS, SEQS, (HEADS + 1) * HD), bf16),
        scratch_shapes=[
            pltpu.VMEM((1, ROWS), jnp.int32),
            pltpu.SMEM((1, ROWS), jnp.int32),
            pltpu.SemaphoreType.DMA,
            pltpu.VMEM((ROWS * SPAN, HD), f32),
            pltpu.VMEM((SEQS * HEADS, HD), f32),
            pltpu.VMEM((SEQS * HEADS, LANES), f32),
        ],
        compiler_params=pltpu.CompilerParams(vmem_limit_bytes=32 << 20),
        name="weigh",
    )(packed, values)


def combine(gathered, out_weight, groups):
    return pl.pallas_call(
        combine_kernel,
        in_specs=[pl.BlockSpec(memory_space=pltpu.VMEM)] * 2,
        out_specs=pl.BlockSpec(memory_space=pltpu.VMEM),
        out_shape=jax.ShapeDtypeStruct((groups, SEQS, LANES), f32),
        name="combine",
    )(gathered, out_weight)


def finish(parts, width):
    return pl.pallas_call(
        finish_kernel,
        in_specs=[pl.BlockSpec(memory_space=pltpu.VMEM)],
        out_specs=pl.BlockSpec(memory_space=pltpu.VMEM),
        out_shape=jax.ShapeDtypeStruct((SEQS, width), bf16),
        name="finish",
    )(parts)


def on_device(query, query_pos, key_latent, key_up, value_cache, chosen, value_slot, out_weight):
    row_table, column_table = angle_tables()
    latent = jnp.swapaxes(key_latent, 1, 2)
    slot_rows = value_slot.reshape(-1, LANES)
    packed = score(query_pos, query, latent, key_up, chosen, slot_rows, row_table, column_table)
    arrived = lax.all_to_all(packed.reshape(POOLS, CAP, LANES), "pool", split_axis=0, concat_axis=0, tiled=True)
    partial = weigh(arrived.reshape(ROWS, LANES), value_cache)
    gathered = lax.all_to_all(partial, "pool", split_axis=0, concat_axis=0, tiled=True)
    groups = lax.axis_size("head")
    projected = combine(gathered, out_weight, groups)
    parts = lax.all_to_all(projected, "head", split_axis=0, concat_axis=0, tiled=True)
    return finish(parts, out_weight.shape[1] // groups)


def solution(mesh):
    placed = (
        P(None, "head"),
        P(),
        P(None, "pool", None),
        P(None, "head"),
        P("pool", None, "head"),
        P(),
        P(),
        P("head", "pool"),
    )
    return jax.shard_map(
        on_device, mesh=mesh, in_specs=placed, out_specs=P(None, ("pool", "head")), check_vma=False
    )
```

time: 417 us -> 72.3 us (0.17)
  blocking collectives: 170 us -> 54.4 us
  local copies, waits for them, and re-layouts: 109 us -> 2.19 us
  waiting for transfers between devices: 73 us -> 0 us
  matrix products: 21.5 us -> 0 us
  Pallas kernels: 0 us -> 15.4 us
  other arithmetic: 14.6 us -> 0 us
  between operations: 13.8 us -> 0.02 us
  starting transfers between devices: 12 us -> 0 us
    psum x1 -> x0, blocking collectives: 110 us -> none  [on_device(): lax.psum(totals.reshape(seq_count, local_heads).astype(jnp.bfloat16), 'po...]
    unnamed x2 -> x0, waiting for transfers between devices: 73 us -> none
    gather x3 -> x0, local copies, waits for them, and re-layouts: 66.7 us -> none  [the longest x1 45.5 us: on_device(): slot_of = value_slot[seq_flat * context_spans + chosen_flat]]
    pmax x1 -> x0, blocking collectives: 60.1 us -> none  [on_device(): global_peak = lax.pmax(local_peak, 'pool')]
    all_to_all x0 -> x3, blocking collectives: none -> 54.4 us  [the longest x1 21.2 us: on_device(): lax.all_to_all(packed.reshape(POOLS, CAP, LANES), 'pool', split_axis=0, c...]
    dot_general x7 -> x0, matrix products: 20.4 us -> none  [the longest x2 14.9 us: compact_rows(): picked = jnp.dot(match_table, facts, precision=lax.Precision.HIGHEST)]
    reshape x3 -> x0, local copies, waits for them, and re-layouts: 19 us -> none  [the longest x1 14.2 us: on_device(): latent_blocks = key_latent.reshape(seq_count, per_holder, SPAN * RANK)]
    pallas_call x0 -> x4, Pallas kernels: none -> 15.4 us  [the longest x1 9.12 us: score(): pl.pallas_call(holder_kernel, in_specs=[pl.BlockSpec(memory_space=pltpu.H...]
  transfers between devices with their start and end apart: 2 -> 0, of which waited for: 1 -> 0; matrix products, arithmetic and copies ran while one was open for 15% -> 0% of each run, Pallas kernels for 0% -> 0%
where the time goes in v1:
time: 72.3 us; the launch traced here: 72 us
  blocking collectives  54.4 us (75%)
  Pallas kernels  15.4 us (21%)
  local copies, waits for them, and re-layouts  2.19 us (3%)
    all_to_all x1, blocking collectives, on_device(): lax.all_to_all(packed.reshape(POOLS, CAP, LANES), 'pool', split_axis=0, c...  21.2 us
    all_to_all x1, blocking collectives, on_device(): lax.all_to_all(partial, 'pool', split_axis=0, concat_axis=0, tiled=True)  19.7 us
    all_to_all x1, blocking collectives, on_device(): lax.all_to_all(projected, 'head', split_axis=0, concat_axis=0, tiled=True)  13.5 us
    pallas_call x1, Pallas kernels, score(): pl.pallas_call(holder_kernel, in_specs=[pl.BlockSpec(memory_space=pltpu.H...  9.12 us
    pallas_call x1, Pallas kernels, combine(): pl.pallas_call(combine_kernel, in_specs=[pl.BlockSpec(memory_space=pltpu....  2.69 us
    pallas_call x1, Pallas kernels, weigh(): pl.pallas_call(owner_kernel, in_specs=[pl.BlockSpec(memory_space=pltpu.VM...  2.2 us
    unnamed x2, local copies, waits for them, and re-layouts  2.19 us

profile of v1, /device:TPU:1, one launch (start us, length us, event | category | flops | bytes accessed | tf_op | source)
XLA Modules:
  0.0 72.0 jit_solution(15352466940393275667)
XLA Ops:
  0.0 9.1 %score.1 = bf16[512,128]{1,0:T(8,128)(2,1)} custom-call(s32[8]{0:T(128)} %pos_hbm.1, bf16[8,1024]{1,0:T(8,128)(2,1)} %query_hbm.1, bf16[8,160,2048]{2,1,0:T(8,128)(2,1)} %bitcast.5, bf16[160,128]{1,0:T(8,128)(2,1)} %key_up_hbm.1, s32[8,1024]{1,0:T(8,128)} %chosen_hbm.1, s32[512,128]{1,0:T(8,128)} %bitcast.7, f32[184,128]{1,0:T(8,128)} %constant.4.clone.row_hbm, ...), custom_call_target="tpu_custom_call" | custom-call | tf_op jit(solution)/shard_map/score/pallas_call | solution.py:337
  9.1 21.2 %all_to_all.15 = bf16[32,16,128]{2,1,0:T(8,128)(2,1)S(1)} all-to-all(bf16[32,16,128]{2,1,0:T(8,128)(2,1)} %bitcast.6), channel_id=1, replica_groups=mesh['pool'=32,'head'=8] {'pool'}, dimensions={0} | all-to-all | bytes 262144 | tf_op jit(solution)/shard_map/all_to_all | solution.py:407
  30.4 0.0 copy-start
  30.4 2.2 %copy-done = bf16[2048,8,128]{2,1,0:T(8,128)(2,1)S(1)} copy-done((bf16[2048,8,128]{2,1,0:T(8,128)(2,1)S(1)}, bf16[2048,8,128]{2,1,0:T(8,128)(2,1)}, u32[]{:S(2)}) %copy-start) | copy-done | bytes 4194328
  32.5 2.2 %weigh.1 = bf16[32,8,1152]{2,1,0:T(8,128)(2,1)S(1)} custom-call(bf16[512,128]{1,0:T(8,128)(2,1)S(1)} %bitcast.4, bf16[2048,8,128]{2,1,0:T(8,128)(2,1)S(1)} %copy-done), custom_call_target="tpu_custom_call" | custom-call | tf_op jit(solution)/shard_map/weigh/pallas_call | solution.py:364
  34.8 19.7 %all_to_all.16.gathered_ref = bf16[32,8,1152]{2,1,0:T(8,128)(2,1)} all-to-all(bf16[32,8,1152]{2,1,0:T(8,128)(2,1)S(1)} %weigh.1), channel_id=1, replica_groups=mesh['pool'=32,'head'=8] {'pool'}, dimensions={0} | all-to-all | bytes 1179648 | tf_op jit(solution)/shard_map/all_to_all | solution.py:409
  54.4 2.7 %combine.1 = f32[8,8,128]{2,1,0:T(8,128)} custom-call(bf16[32,8,1152]{2,1,0:T(8,128)(2,1)} %all_to_all.16.gathered_ref, bf16[1024,256]{1,0:T(8,128)(2,1)} %weight_ref.1), custom_call_target="tpu_custom_call" | custom-call | tf_op jit(solution)/shard_map/combine/pallas_call | solution.py:383
  57.1 13.5 %all_to_all.17.parts_ref = f32[8,8,128]{2,1,0:T(8,128)} all-to-all(f32[8,8,128]{2,1,0:T(8,128)} %combine.1), channel_id=1, replica_groups=mesh['pool'=32,'head'=8] {'head'}, dimensions={0} | all-to-all | bytes 65536 | tf_op jit(solution)/shard_map/all_to_all | solution.py:412
  70.6 1.3 %finish.1 = bf16[8,32]{1,0:T(8,128)(2,1)} custom-call(f32[8,8,128]{2,1,0:T(8,128)} %all_to_all.17.parts_ref), custom_call_target="tpu_custom_call" | custom-call | tf_op jit(solution)/shard_map/finish/pallas_call | solution.py:393
Async XLA Ops:
  30.4 2.2 %copy-start = (bf16[2048,8,128]{2,1,0:T(8,128)(2,1)S(1)}, bf16[2048,8,128]{2,1,0:T(8,128)(2,1)}, u32[]{:S(2)}) copy-start(bf16[2048,8,128]{2,1,0:T(8,128)(2,1)} %values_ref.1) | copy-start | bytes 12582916

commit v2 on v1

--- a/solution.py
+++ b/solution.py
@@ -103,7 +103,7 @@
         sin_scr[:, c * LANES : (c + 1) * LANES] = sa * c3 + ca * s3
 
 
-def plan(pool, chosen_ref, slot_ref, slot_scr, span_scr, seq_scr, meta_scr):
+def plan(pool, chosen_ref, slot_ref, slot_scr, span_scr, seq_scr, meta_scr, mask_scr):
     relative = chosen_ref[...] - pool * SPANS
     here = (relative >= 0) & (relative < SPANS)
     row_code = jnp.where(here, 2 * iota(relative.shape, 0) + (relative >> 7), -1)
@@ -114,6 +114,7 @@
         left = onehot(iota((CHUNKS, picks), 0) == row_code[s : s + 1, :])
         right = onehot(iota((LANES, picks), 0) == lane_code[s : s + 1, :])
         member = member + dot_nt(left, right)
+    mask_scr[...] = dot(member.astype(bf16), onehot(iota((LANES, LANES * SPAN), 0) == (iota((LANES, LANES * SPAN), 1) >> 3)))
     for s in range(SEQS):
         slot_scr[2 * s : 2 * s + 2, :] = slot_ref[pl.ds(s * (SPANS * POOLS // LANES) + 2 * pool, 2), :]
     slots = slot_scr[...]
@@ -162,43 +163,43 @@
     meta_scr[...] = known[:, 2 * LANES :]
 
 
-def pack_rows(score_scr, turned_scr, span_scr, seq_scr, meta_scr, out_ref):
-    scores = score_scr[...]
-    first = scores.astype(bf16).astype(f32)
-    turned_scr[...] = jnp.concatenate([first, scores - first], axis=0).T
-    parts = [turned_scr[pl.ds(t, SPANS, stride=SPAN), :].astype(bf16) for t in range(SPAN)]
-    by_span = jnp.concatenate(parts, axis=1)
-    width = SPAN * LANES
+def pack_rows(score_scr, turned_scr, levels, span_scr, seq_scr, meta_scr, out_ref):
+    weights = score_scr[...]
+    turned_scr[...] = jnp.concatenate([weights, weights], axis=0).T
+    low = iota((SPANS, LANES), 1) < 64
+    parts = [
+        jnp.where(low, turned_scr[pl.ds(t, SPANS, stride=SPAN), :], turned_scr[pl.ds(t + 1, SPANS, stride=SPAN), :])
+        for t in range(0, SPAN, 2)
+    ]
+    by_span = jnp.concatenate(parts, axis=1).astype(bf16)
+    width = by_span.shape[1]
     source = iota((width, LANES), 0)
     target = iota((width, LANES), 1)
-    fold = onehot(((source >> 7) == ((target & 63) >> 3)) & ((source & 7) == (target & 7)))
+    fold = onehot((target < 64) & ((source >> 6) == (target >> 3)) & ((source & 7) == (target & 7)))
+    first, second, third = pieces_of(levels)
+    own = jnp.concatenate([first, second, third], axis=0)
+    gap = jnp.zeros((8, LANES), f32)
+    table = jnp.concatenate([gap] * 8 + [own, gap, pltpu.roll(own, 8, 1), gap], axis=0).astype(bf16)
     block = 128
     lane = iota((block, LANES), 1)
     lane_seq = ((lane & 63) >> 3).astype(f32) + 1.0
+    rank = iota((block, LANES), 0) & (CAP - 1)
     for start in range(0, ROWS, block):
         span = span_scr[start : start + block, :]
         seq = seq_scr[start : start + block, :]
         pick = jnp.concatenate([onehot(lane.astype(f32) == span), onehot((lane + LANES).astype(f32) == span)], axis=1)
         found = dot(pick, by_span)
         mine = seq == lane_seq
-        kept = [jnp.where(mine, found[:, t * LANES : (t + 1) * LANES], 0.0) for t in range(SPAN)]
-        score = dot(jnp.concatenate(kept, axis=1).astype(bf16), fold) * (1.0 / math.sqrt(HD))
-        peak = score
-        for shift in (8, 16, 32):
-            peak = jnp.maximum(peak, pltpu.roll(peak, shift, 1))
-        weight = jnp.where(seq > 0.5, jnp.exp(score - peak), 0.0)
-        one, two, three = pieces_of(peak)
-        packed = jnp.where(lane < 88, three, meta_scr[start : start + block, :])
-        packed = jnp.where(lane < 80, two, packed)
-        packed = jnp.where(lane < 72, one, packed)
-        packed = jnp.where(lane < 64, weight, packed)
-        out_ref[start : start + block, :] = packed.astype(bf16)
+        kept = [jnp.where(mine, found[:, i : i + LANES], 0.0) for i in range(0, width, LANES)]
+        chooser = onehot(((lane < 8) & (seq == (lane + 1).astype(f32))) | ((lane >= 8) & (lane < 16) & (rank == lane - 8)))
+        packed = dot(jnp.concatenate(kept, axis=1).astype(bf16), fold) + dot_nt(chooser, table)
+        out_ref[start : start + block, :] = (packed + meta_scr[start : start + block, :]).astype(bf16)
 
 
 def holder_kernel(
     pos_hbm, query_hbm, latent_hbm, key_up_hbm, chosen_hbm, slot_hbm, row_hbm, column_hbm, out_ref,
     pos_ref, query_ref, latent_ref, key_up_ref, chosen_ref, slot_ref, row_ref, column_ref, sems,
-    angle_scr, q_scr, q_out, up_scr, cos_scr, sin_scr, slot_scr, span_scr, seq_scr, meta_scr, score_scr, turned_scr,
+    angle_scr, q_scr, q_out, up_scr, cos_scr, sin_scr, slot_scr, span_scr, seq_scr, meta_scr, mask_scr, score_scr, turned_scr,
 ):
     small = [
         pltpu.make_async_copy(source, target, sems.at[i])
@@ -222,49 +223,56 @@
     for copy in small:
         copy.wait()
     pool = lax.axis_index("pool")
-    plan(pool, chosen_ref, slot_ref, slot_scr, span_scr, seq_scr, meta_scr)
+    plan(pool, chosen_ref, slot_ref, slot_scr, span_scr, seq_scr, meta_scr, mask_scr)
     rotate_queries(pos_ref, query_ref, row_ref, angle_scr, q_scr, q_out)
     key_angles(pool, column_ref, cos_scr, sin_scr)
     up_scr[...] = key_up_ref[...].astype(f32).T.astype(bf16)
-    score_all(latents, latent_ref, up_scr, q_out, cos_scr, sin_scr, score_scr)
-    pack_rows(score_scr, turned_scr, span_scr, seq_scr, meta_scr, out_ref)
-
-
-def score_all(latents, latent_ref, up_scr, q_out, cos_scr, sin_scr, score_scr):
+    for copy in latents:
+        copy.wait()
+    levels = score_all(latents, latent_ref, up_scr, q_out, cos_scr, sin_scr, mask_scr, score_scr)
+    pack_rows(score_scr, turned_scr, levels, span_scr, seq_scr, meta_scr, out_ref)
+
+
+def score_all(latents, latent_ref, up_scr, q_out, cos_scr, sin_scr, mask_scr, score_scr):
     up = up_scr[...]
     cosine, sine = cos_scr[...], sin_scr[...]
-    for s in range(SEQS):
-        latents[s].wait()
+    lane = iota((HEADS, LANES), 1)
+    levels = jnp.zeros((HEADS, LANES), f32)
+    for s in range(SEQS):
         keys = dot(up, latent_ref[s])
         a, b = keys[:HALF], keys[HALF:]
         turned = jnp.concatenate([a * cosine - b * sine, b * cosine + a * sine], axis=0).astype(bf16)
-        score_scr[s * HEADS : (s + 1) * HEADS, :] = dot(q_out[s].astype(bf16), turned)
-
-
-def owner_kernel(
-    packed_ref, values_ref, out_ref, slot_vec, slot_sca, sem, found_scr, sum_scr, level_scr
-):
+        scores = dot(q_out[s].astype(bf16), turned) * (1.0 / math.sqrt(HD))
+        live = jnp.concatenate([mask_scr[2 * s : 2 * s + 1, :], mask_scr[2 * s + 1 : 2 * s + 2, :]], axis=1) > 0.5
+        peak = jnp.max(jnp.where(live, scores, BIG_NEG), axis=1, keepdims=True)
+        weights = jnp.where(live, jnp.exp(scores - peak), 0.0)
+        total = jnp.sum(weights, axis=1, keepdims=True)
+        some = total > 0.0
+        safe = jnp.where(some, total, 1.0)
+        score_scr[s * HEADS : (s + 1) * HEADS, :] = weights * (1.0 / safe)
+        levels = jnp.where(lane == s, jnp.where(some, peak + jnp.log(safe), BIG_NEG), levels)
+    return levels
+
+
+def owner_kernel(packed_ref, values_ref, out_ref, slot_vec, slot_sca, sem, found_scr, sum_scr):
     packed = packed_ref[...].astype(f32).T
     slot_vec[...] = (packed[88:89] * 64.0 + packed[89:90]).astype(jnp.int32)
     copy = pltpu.make_async_copy(slot_vec, slot_sca, sem)
     copy.start()
     seq = packed[90:91]
     live = seq > 0.5
-    peak = jnp.where(live, packed[64:72] + packed[72:80] + packed[80:88], BIG_NEG)
     mine = [seq == float(s + 1) for s in range(SEQS)]
-    tops = [jnp.max(jnp.where(mine[s], peak, BIG_NEG), axis=1, keepdims=True) for s in range(SEQS)]
-    top = jnp.zeros_like(peak)
-    for s in range(SEQS):
-        top = jnp.where(mine[s], tops[s], top)
-    factor = jnp.where(live, jnp.exp(peak - top), 0.0)
-    weights = [(packed[t * HEADS : (t + 1) * HEADS] * factor).astype(bf16).astype(f32) for t in range(SPAN)]
-    over_span = weights[0]
-    for t in range(1, SPAN):
-        over_span = over_span + weights[t]
-    totals = jnp.concatenate(
-        [jnp.sum(jnp.where(mine[s], over_span, 0.0), axis=1, keepdims=True) for s in range(SEQS)], axis=0
-    )
-    peaks = jnp.concatenate(tops, axis=0)
+    level = packed[64:72] + packed[72:80] + packed[80:88]
+    every = packed[96:104] + packed[104:112] + packed[112:120]
+    rank = iota((1, ROWS), 1) & (CAP - 1)
+    level_of = jnp.zeros_like(level)
+    for s in range(SEQS):
+        here = rank == s
+        top = jnp.max(jnp.where(here, every, BIG_NEG), axis=1, keepdims=True)
+        total = jnp.sum(jnp.where(here, jnp.exp(every - top), 0.0), axis=1, keepdims=True)
+        level_of = jnp.where(mine[s], top + jnp.log(total), level_of)
+    factor = jnp.where(live, jnp.exp(level - level_of), 0.0)
+    weights = [packed[t * HEADS : (t + 1) * HEADS] * factor for t in range(SPAN)]
     copy.wait()
 
     @pl.loop(0, ROWS // 16)
@@ -278,44 +286,17 @@
         left = jnp.concatenate([jnp.where(mine[s], weights[t], 0.0) for s in range(SEQS)], axis=0).astype(bf16)
         right = found_scr[pl.ds(t, ROWS, stride=SPAN), :].astype(bf16)
         summed = summed + dot(left, right)
-    some = totals > 0.0
-    safe = jnp.where(some, totals, 1.0)
-    sum_scr[...] = summed / safe
-    level = jnp.where(some, peaks + jnp.log(safe), BIG_NEG)
-    level_scr[...] = jnp.broadcast_to(level, level_scr.shape)
-    lane = iota((SEQS, LANES), 1)
-    tail = jnp.zeros((SEQS, LANES), f32)
-    parts = []
-    for h in range(HEADS):
-        parts.append(sum_scr[pl.ds(h, SEQS, stride=HEADS), :])
-        tail = jnp.where((lane & 7) == h, level_scr[pl.ds(h, SEQS, stride=HEADS), :], tail)
-    one, two, three = pieces_of(tail)
-    parts.append(jnp.where(lane < 8, one, jnp.where(lane < 16, two, jnp.where(lane < 24, three, 0.0))))
-    result = jnp.concatenate(parts, axis=1).astype(bf16)
+    sum_scr[...] = summed
+    result = jnp.concatenate([sum_scr[pl.ds(h, SEQS, stride=HEADS), :] for h in range(HEADS)], axis=1).astype(bf16)
     for p in range(POOLS):
         out_ref[p] = result
 
 
 def combine_kernel(gathered_ref, weight_ref, out_ref):
-    levels = []
-    for p in range(POOLS):
-        tail = gathered_ref[p, :, HEADS * HD :].astype(f32)
-        levels.append(tail + pltpu.roll(tail, LANES - 8, 1) + pltpu.roll(tail, LANES - 16, 1))
-    top = levels[0]
+    total = gathered_ref[0].astype(f32)
     for p in range(1, POOLS):
-        top = jnp.maximum(top, levels[p])
-    shares = [jnp.exp(level - top) for level in levels]
-    total = shares[0]
-    for p in range(1, POOLS):
-        total = total + shares[p]
-    inverse = 1.0 / total
-    sums = [jnp.zeros((SEQS, HD), f32) for _ in range(HEADS)]
-    for p in range(POOLS):
-        share = shares[p] * inverse
-        for h in range(HEADS):
-            sums[h] = sums[h] + share[:, h : h + 1] * gathered_ref[p, :, h * HD : (h + 1) * HD].astype(f32)
-    attended = jnp.concatenate(sums, axis=1).astype(bf16)
-    projected = dot(attended, weight_ref[...])
+        total = total + gathered_ref[p].astype(f32)
+    projected = dot(total.astype(bf16), weight_ref[...])
     groups = out_ref.shape[0]
     width = projected.shape[1] // groups
     for g in range(groups):
@@ -352,12 +333,13 @@
             pltpu.VMEM((ROWS, LANES), f32),
             pltpu.VMEM((ROWS, LANES), f32),
             pltpu.VMEM((ROWS, LANES), f32),
+            pltpu.VMEM((CHUNKS, LANES * SPAN), f32),
             pltpu.VMEM((SEQS * HEADS, TOKENS), f32),
             pltpu.VMEM((TOKENS, LANES), f32),
         ],
-        compiler_params=pltpu.CompilerParams(vmem_limit_bytes=63_400_000),
+        compiler_params=pltpu.CompilerParams(vmem_limit_bytes=32 << 20),
         name="score",
-    )(*operands)
+    )(*[pltpu.with_memory_space_constraint(x, pltpu.HBM) for x in operands])
 
 
 def weigh(packed, values):
@@ -365,16 +347,15 @@
         owner_kernel,
         in_specs=[pl.BlockSpec(memory_space=pltpu.VMEM)] * 2,
         out_specs=pl.BlockSpec(memory_space=pltpu.VMEM),
-        out_shape=jax.ShapeDtypeStruct((POOLS, SEQS, (HEADS + 1) * HD), bf16),
+        out_shape=jax.ShapeDtypeStruct((POOLS, SEQS, HEADS * HD), bf16),
         scratch_shapes=[
             pltpu.VMEM((1, ROWS), jnp.int32),
             pltpu.SMEM((1, ROWS), jnp.int32),
             pltpu.SemaphoreType.DMA,
             pltpu.VMEM((ROWS * SPAN, HD), f32),
             pltpu.VMEM((SEQS * HEADS, HD), f32),
-            pltpu.VMEM((SEQS * HEADS, LANES), f32),
         ],
-        compiler_params=pltpu.CompilerParams(vmem_limit_bytes=32 << 20),
+        compiler_params=pltpu.CompilerParams(vmem_limit_bytes=24 << 20),
         name="weigh",
     )(packed, values)
 
@@ -385,6 +366,7 @@
         in_specs=[pl.BlockSpec(memory_space=pltpu.VMEM)] * 2,
         out_specs=pl.BlockSpec(memory_space=pltpu.VMEM),
         out_shape=jax.ShapeDtypeStruct((groups, SEQS, LANES), f32),
+        compiler_params=pltpu.CompilerParams(vmem_limit_bytes=16 << 20),
         name="combine",
     )(gathered, out_weight)
 
@@ -395,6 +377,7 @@
         in_specs=[pl.BlockSpec(memory_space=pltpu.VMEM)],
         out_specs=pl.BlockSpec(memory_space=pltpu.VMEM),
         out_shape=jax.ShapeDtypeStruct((SEQS, width), bf16),
+        compiler_params=pltpu.CompilerParams(vmem_limit_bytes=8 << 20),
         name="finish",
     )(parts)
 

time: 72.3 us -> 62.9 us (0.87)
  Pallas kernels: 15.4 us -> 10.6 us
  blocking collectives: 54.4 us -> 52.1 us
  local copies, waits for them, and re-layouts: 2.19 us -> 0.01 us
    pallas_call x1, Pallas kernels: 2.69 us -> 0.29 us  [combine(): pl.pallas_call(combine_kernel, in_specs=[pl.BlockSpec(memory_space=pltpu....]
    unnamed x2 -> x4, local copies, waits for them, and re-layouts: 2.19 us -> 0.01 us
    pallas_call x1, Pallas kernels: 9.12 us -> 7.57 us  [score(): pl.pallas_call(holder_kernel, in_specs=[pl.BlockSpec(memory_space=pltpu.H...]
    all_to_all x1, blocking collectives: 19.7 us -> 18.2 us  [on_device(): lax.all_to_all(partial, 'pool', split_axis=0, concat_axis=0, tiled=True)]
    pallas_call x1, Pallas kernels: 1.34 us -> 0.59 us  [finish(): pl.pallas_call(finish_kernel, in_specs=[pl.BlockSpec(memory_space=pltpu.V...]
where the time goes in v2:
time: 62.9 us; the launch traced here: 62.8 us
  blocking collectives  52.1 us (83%)
  Pallas kernels  10.6 us (17%)
    all_to_all x1, blocking collectives, on_device(): lax.all_to_all(packed.reshape(POOLS, CAP, LANES), 'pool', split_axis=0, c...  21 us
    all_to_all x1, blocking collectives, on_device(): lax.all_to_all(partial, 'pool', split_axis=0, concat_axis=0, tiled=True)  18.2 us
    all_to_all x1, blocking collectives, on_device(): lax.all_to_all(projected, 'head', split_axis=0, concat_axis=0, tiled=True)  12.9 us
    pallas_call x1, Pallas kernels, score(): pl.pallas_call(holder_kernel, in_specs=[pl.BlockSpec(memory_space=pltpu.H...  7.57 us
    pallas_call x1, Pallas kernels, weigh(): pl.pallas_call(owner_kernel, in_specs=[pl.BlockSpec(memory_space=pltpu.VM...  2.19 us

profile of v2, /device:TPU:1, one launch (start us, length us, event | category | flops | bytes accessed | tf_op | source)
XLA Modules:
  0.0 62.8 jit_solution(2626013545750852576)
XLA Ops:
  0.0 0.0 copy-start
  0.0 0.0 copy-start.1
  0.0 7.6 %score.1 = bf16[512,128]{1,0:T(8,128)(2,1)S(1)} custom-call(s32[8]{0:T(128)} %pos_hbm.1, bf16[8,1024]{1,0:T(8,128)(2,1)} %query_hbm.1, bf16[8,160,2048]{2,1,0:T(8,128)(2,1)} %bitcast.6, bf16[160,128]{1,0:T(8,128)(2,1)} %key_up_hbm.1, s32[8,1024]{1,0:T(8,128)} %chosen_hbm.1, s32[512,128]{1,0:T(8,128)} %bitcast.7, f32[184,128]{1,0:T(8,128)} %constant.4.clone.row_hbm, ...), custom_call_target="tpu_custom_call" | custom-call | tf_op jit(solution)/shard_map/score/pallas_call | solution.py:318
  7.6 21.0 %all_to_all.15 = bf16[32,16,128]{2,1,0:T(8,128)(2,1)S(1)} all-to-all(bf16[32,16,128]{2,1,0:T(8,128)(2,1)S(1)} %bitcast.4), channel_id=1, replica_groups=mesh['pool'=32,'head'=8] {'pool'}, dimensions={0} | all-to-all | bytes 262144 | tf_op jit(solution)/shard_map/all_to_all | solution.py:390
  28.6 0.0 copy-done
  28.6 2.2 %weigh.1 = bf16[32,8,1024]{2,1,0:T(8,128)(2,1)S(1)} custom-call(bf16[512,128]{1,0:T(8,128)(2,1)S(1)} %bitcast.5, bf16[2048,8,128]{2,1,0:T(8,128)(2,1)S(1)} %copy-done), custom_call_target="tpu_custom_call" | custom-call | tf_op jit(solution)/shard_map/weigh/pallas_call | solution.py:346
  30.8 18.2 %all_to_all.16.gathered_ref = bf16[32,8,1024]{2,1,0:T(8,128)(2,1)S(1)} all-to-all(bf16[32,8,1024]{2,1,0:T(8,128)(2,1)S(1)} %weigh.1), channel_id=1, replica_groups=mesh['pool'=32,'head'=8] {'pool'}, dimensions={0} | all-to-all | bytes 1048576 | tf_op jit(solution)/shard_map/all_to_all | solution.py:392
  49.0 0.0 copy-done.1
  49.0 0.3 combine.1
  49.3 12.9 %all_to_all.17.parts_ref = f32[8,8,128]{2,1,0:T(8,128)S(1)} all-to-all(f32[8,8,128]{2,1,0:T(8,128)S(1)} %combine.1), channel_id=1, replica_groups=mesh['pool'=32,'head'=8] {'head'}, dimensions={0} | all-to-all | bytes 65536 | tf_op jit(solution)/shard_map/all_to_all | solution.py:395
  62.2 0.6 finish.1
Async XLA Ops:
  0.0 28.6 %copy-start = (bf16[2048,8,128]{2,1,0:T(8,128)(2,1)S(1)}, bf16[2048,8,128]{2,1,0:T(8,128)(2,1)}, u32[]{:S(2)}) copy-start(bf16[2048,8,128]{2,1,0:T(8,128)(2,1)} %values_ref.1) | copy-start | bytes 12582916
  0.0 49.0 %copy-start.1 = (bf16[1024,256]{1,0:T(8,128)(2,1)S(1)}, bf16[1024,256]{1,0:T(8,128)(2,1)}, u32[]{:S(2)}) copy-start(bf16[1024,256]{1,0:T(8,128)(2,1)} %weight_ref.1) | copy-start | bytes 1572868

commit v3 on v2

--- a/solution.py
+++ b/solution.py
@@ -6,6 +6,7 @@
 from jax import lax
 from jax.experimental import pallas as pl
 from jax.experimental.pallas import tpu as pltpu
+from jax.sharding import Mesh
 from jax.sharding import PartitionSpec as P
 
 SEQS = 8
@@ -18,6 +19,7 @@
 LANES = 128
 
 POOLS = 32
+PAIRS = POOLS // 2
 CAP = 16
 ROWS = POOLS * CAP
 SPANS = 256
@@ -109,11 +111,9 @@
     row_code = jnp.where(here, 2 * iota(relative.shape, 0) + (relative >> 7), -1)
     lane_code = relative & 127
     picks = relative.shape[1]
-    member = jnp.zeros((CHUNKS, LANES), f32)
-    for s in range(SEQS):
-        left = onehot(iota((CHUNKS, picks), 0) == row_code[s : s + 1, :])
-        right = onehot(iota((LANES, picks), 0) == lane_code[s : s + 1, :])
-        member = member + dot_nt(left, right)
+    left = [onehot(iota((CHUNKS, picks), 0) == row_code[s : s + 1, :]) for s in range(SEQS)]
+    right = [onehot(iota((LANES, picks), 0) == lane_code[s : s + 1, :]) for s in range(SEQS)]
+    member = dot_nt(jnp.concatenate(left, axis=1), jnp.concatenate(right, axis=1))
     mask_scr[...] = dot(member.astype(bf16), onehot(iota((LANES, LANES * SPAN), 0) == (iota((LANES, LANES * SPAN), 1) >> 3)))
     for s in range(SEQS):
         slot_scr[2 * s : 2 * s + 2, :] = slot_ref[pl.ds(s * (SPANS * POOLS // LANES) + 2 * pool, 2), :]
@@ -179,27 +179,26 @@
     first, second, third = pieces_of(levels)
     own = jnp.concatenate([first, second, third], axis=0)
     gap = jnp.zeros((8, LANES), f32)
-    table = jnp.concatenate([gap] * 8 + [own, gap, pltpu.roll(own, 8, 1), gap], axis=0).astype(bf16)
-    block = 128
-    lane = iota((block, LANES), 1)
+    table = jnp.concatenate([gap] * 8 + [own, gap, pltpu.roll(own, 8, 1), gap], axis=0)
+    fold = jnp.concatenate([fold, table.T.astype(bf16)], axis=0)
+    lane = iota((ROWS, LANES), 1)
     lane_seq = ((lane & 63) >> 3).astype(f32) + 1.0
-    rank = iota((block, LANES), 0) & (CAP - 1)
-    for start in range(0, ROWS, block):
-        span = span_scr[start : start + block, :]
-        seq = seq_scr[start : start + block, :]
-        pick = jnp.concatenate([onehot(lane.astype(f32) == span), onehot((lane + LANES).astype(f32) == span)], axis=1)
-        found = dot(pick, by_span)
-        mine = seq == lane_seq
-        kept = [jnp.where(mine, found[:, i : i + LANES], 0.0) for i in range(0, width, LANES)]
-        chooser = onehot(((lane < 8) & (seq == (lane + 1).astype(f32))) | ((lane >= 8) & (lane < 16) & (rank == lane - 8)))
-        packed = dot(jnp.concatenate(kept, axis=1).astype(bf16), fold) + dot_nt(chooser, table)
-        out_ref[start : start + block, :] = (packed + meta_scr[start : start + block, :]).astype(bf16)
+    rank = iota((ROWS, LANES), 0) & (CAP - 1)
+    span = span_scr[...]
+    seq = seq_scr[...]
+    pick = jnp.concatenate([onehot(lane.astype(f32) == span), onehot((lane + LANES).astype(f32) == span)], axis=1)
+    chooser = onehot(((lane < 8) & (seq == (lane + 1).astype(f32))) | ((lane >= 8) & (lane < 16) & (rank == lane - 8)))
+    found = dot(pick, by_span)
+    mine = seq == lane_seq
+    kept = [jnp.where(mine, found[:, i : i + LANES], 0.0).astype(bf16) for i in range(0, width, LANES)]
+    packed = dot(jnp.concatenate(kept + [chooser], axis=1), fold)
+    out_ref[...] = (packed + meta_scr[...]).astype(bf16)
 
 
 def holder_kernel(
     pos_hbm, query_hbm, latent_hbm, key_up_hbm, chosen_hbm, slot_hbm, row_hbm, column_hbm, out_ref,
     pos_ref, query_ref, latent_ref, key_up_ref, chosen_ref, slot_ref, row_ref, column_ref, sems,
-    angle_scr, q_scr, q_out, up_scr, cos_scr, sin_scr, slot_scr, span_scr, seq_scr, meta_scr, mask_scr, score_scr, turned_scr,
+    angle_scr, q_scr, q_out, up_scr, cos_scr, sin_scr, slot_scr, span_scr, seq_scr, meta_scr, mask_scr, score_scr, turned_scr, turned_keys,
 ):
     small = [
         pltpu.make_async_copy(source, target, sems.at[i])
@@ -222,27 +221,34 @@
         copy.start()
     for copy in small:
         copy.wait()
-    pool = lax.axis_index("pool")
+    pool = lax.axis_index("pair") * 2 + lax.axis_index("side")
     plan(pool, chosen_ref, slot_ref, slot_scr, span_scr, seq_scr, meta_scr, mask_scr)
     rotate_queries(pos_ref, query_ref, row_ref, angle_scr, q_scr, q_out)
     key_angles(pool, column_ref, cos_scr, sin_scr)
     up_scr[...] = key_up_ref[...].astype(f32).T.astype(bf16)
     for copy in latents:
         copy.wait()
-    levels = score_all(latents, latent_ref, up_scr, q_out, cos_scr, sin_scr, mask_scr, score_scr)
+    levels = score_all(turned_keys, latent_ref, up_scr, q_out, cos_scr, sin_scr, mask_scr, score_scr)
     pack_rows(score_scr, turned_scr, levels, span_scr, seq_scr, meta_scr, out_ref)
 
 
-def score_all(latents, latent_ref, up_scr, q_out, cos_scr, sin_scr, mask_scr, score_scr):
+def score_all(turned_keys, latent_ref, up_scr, q_out, cos_scr, sin_scr, mask_scr, score_scr):
     up = up_scr[...]
     cosine, sine = cos_scr[...], sin_scr[...]
     lane = iota((HEADS, LANES), 1)
     levels = jnp.zeros((HEADS, LANES), f32)
     for s in range(SEQS):
-        keys = dot(up, latent_ref[s])
-        a, b = keys[:HALF], keys[HALF:]
-        turned = jnp.concatenate([a * cosine - b * sine, b * cosine + a * sine], axis=0).astype(bf16)
-        scores = dot(q_out[s].astype(bf16), turned) * (1.0 / math.sqrt(HD))
+        for at in range(0, TOKENS, 256):
+            keys = dot(up, latent_ref[s, :, at : at + 256])
+            a, b = keys[:HALF], keys[HALF:]
+            co, si = cos_scr[:, at : at + 256], sin_scr[:, at : at + 256]
+            turned_keys[s * HD : s * HD + HALF, at : at + 256] = (a * co - b * si).astype(bf16)
+            turned_keys[s * HD + HALF : (s + 1) * HD, at : at + 256] = (b * co + a * si).astype(bf16)
+    gap = jnp.zeros((HEADS, HD), f32)
+    spread = [jnp.concatenate([q_out[s] if i == s else gap for i in range(SEQS)], axis=1) for s in range(SEQS)]
+    every = dot(jnp.concatenate(spread, axis=0).astype(bf16), turned_keys[...]) * (1.0 / math.sqrt(HD))
+    for s in range(SEQS):
+        scores = every[s * HEADS : (s + 1) * HEADS]
         live = jnp.concatenate([mask_scr[2 * s : 2 * s + 1, :], mask_scr[2 * s + 1 : 2 * s + 2, :]], axis=1) > 0.5
         peak = jnp.max(jnp.where(live, scores, BIG_NEG), axis=1, keepdims=True)
         weights = jnp.where(live, jnp.exp(scores - peak), 0.0)
@@ -281,28 +287,29 @@
             row = step * 16 + i
             found_scr[pl.ds(pl.multiple_of(row * SPAN, SPAN), SPAN), :] = values_ref[slot_sca[0, row]].astype(f32)
 
-    summed = jnp.zeros((SEQS * HEADS, HD), f32)
-    for t in range(SPAN):
-        left = jnp.concatenate([jnp.where(mine[s], weights[t], 0.0) for s in range(SEQS)], axis=0).astype(bf16)
-        right = found_scr[pl.ds(t, ROWS, stride=SPAN), :].astype(bf16)
-        summed = summed + dot(left, right)
-    sum_scr[...] = summed
+    left = [jnp.concatenate([jnp.where(mine[s], weights[t], 0.0) for s in range(SEQS)], axis=0).astype(bf16) for t in range(SPAN)]
+    right = [found_scr[pl.ds(t, ROWS, stride=SPAN), :].astype(bf16) for t in range(SPAN)]
+    sum_scr[...] = dot(jnp.concatenate(left, axis=1), jnp.concatenate(right, axis=0))
     result = jnp.concatenate([sum_scr[pl.ds(h, SEQS, stride=HEADS), :] for h in range(HEADS)], axis=1).astype(bf16)
-    for p in range(POOLS):
+    for p in range(PAIRS):
         out_ref[p] = result
 
 
-def combine_kernel(gathered_ref, weight_ref, out_ref):
+def combine_kernel(gathered_ref, *refs):
+    *weight_refs, out_ref = refs
     total = gathered_ref[0].astype(f32)
-    for p in range(1, POOLS):
+    for p in range(1, PAIRS):
         total = total + gathered_ref[p].astype(f32)
-    projected = dot(total.astype(bf16), weight_ref[...])
-    groups = out_ref.shape[0]
-    width = projected.shape[1] // groups
-    for g in range(groups):
-        at = g * width
-        half = projected[:, at // LANES * LANES : (at // LANES + 1) * LANES]
-        out_ref[g] = pltpu.roll(half, (LANES - at % LANES) % LANES, 1)
+    total = total.astype(bf16)
+    side = lax.axis_index("side")
+    groups = out_ref.shape[0] // 2
+    for k in range(2):
+        projected = dot(total, weight_refs[k][...])
+        width = projected.shape[1] // groups
+        for g in range(groups):
+            at = g * width
+            half = projected[:, at // LANES * LANES : (at // LANES + 1) * LANES]
+            out_ref[(side ^ k) * groups + g] = pltpu.roll(half, (LANES - at % LANES) % LANES, 1)
 
 
 def finish_kernel(parts_ref, out_ref):
@@ -336,6 +343,7 @@
             pltpu.VMEM((CHUNKS, LANES * SPAN), f32),
             pltpu.VMEM((SEQS * HEADS, TOKENS), f32),
             pltpu.VMEM((TOKENS, LANES), f32),
+            pltpu.VMEM((SEQS * HD, TOKENS), bf16),
         ],
         compiler_params=pltpu.CompilerParams(vmem_limit_bytes=32 << 20),
         name="score",
@@ -347,7 +355,7 @@
         owner_kernel,
         in_specs=[pl.BlockSpec(memory_space=pltpu.VMEM)] * 2,
         out_specs=pl.BlockSpec(memory_space=pltpu.VMEM),
-        out_shape=jax.ShapeDtypeStruct((POOLS, SEQS, HEADS * HD), bf16),
+        out_shape=jax.ShapeDtypeStruct((PAIRS, SEQS, HEADS * HD), bf16),
         scratch_shapes=[
             pltpu.VMEM((1, ROWS), jnp.int32),
             pltpu.SMEM((1, ROWS), jnp.int32),
@@ -360,15 +368,15 @@
     )(packed, values)
 
 
-def combine(gathered, out_weight, groups):
+def combine(gathered, weights, groups):
     return pl.pallas_call(
         combine_kernel,
-        in_specs=[pl.BlockSpec(memory_space=pltpu.VMEM)] * 2,
+        in_specs=[pl.BlockSpec(memory_space=pltpu.VMEM)] * 3,
         out_specs=pl.BlockSpec(memory_space=pltpu.VMEM),
-        out_shape=jax.ShapeDtypeStruct((groups, SEQS, LANES), f32),
+        out_shape=jax.ShapeDtypeStruct((2 * groups, SEQS, LANES), f32),
         compiler_params=pltpu.CompilerParams(vmem_limit_bytes=16 << 20),
         name="combine",
-    )(gathered, out_weight)
+    )(gathered, *weights)
 
 
 def finish(parts, width):
@@ -386,27 +394,30 @@
     row_table, column_table = angle_tables()
     latent = jnp.swapaxes(key_latent, 1, 2)
     slot_rows = value_slot.reshape(-1, LANES)
+    weights = [out_weight, lax.ppermute(out_weight, "side", [(0, 1), (1, 0)])]
     packed = score(query_pos, query, latent, key_up, chosen, slot_rows, row_table, column_table)
-    arrived = lax.all_to_all(packed.reshape(POOLS, CAP, LANES), "pool", split_axis=0, concat_axis=0, tiled=True)
+    arrived = lax.all_to_all(packed.reshape(POOLS, CAP, LANES), ("pair", "side"), split_axis=0, concat_axis=0, tiled=True)
+    arrived, weights[1] = lax.optimization_barrier((arrived, weights[1]))
     partial = weigh(arrived.reshape(ROWS, LANES), value_cache)
-    gathered = lax.all_to_all(partial, "pool", split_axis=0, concat_axis=0, tiled=True)
+    gathered = lax.all_to_all(partial, "pair", split_axis=0, concat_axis=0, tiled=True)
     groups = lax.axis_size("head")
-    projected = combine(gathered, out_weight, groups)
-    parts = lax.all_to_all(projected, "head", split_axis=0, concat_axis=0, tiled=True)
+    projected = combine(gathered, weights, groups)
+    parts = lax.all_to_all(projected, ("side", "head"), split_axis=0, concat_axis=0, tiled=True)
     return finish(parts, out_weight.shape[1] // groups)
 
 
 def solution(mesh):
+    split = Mesh(mesh.devices.reshape(PAIRS, 2, -1), ("pair", "side", "head"))
     placed = (
         P(None, "head"),
         P(),
-        P(None, "pool", None),
+        P(None, ("pair", "side"), None),
         P(None, "head"),
-        P("pool", None, "head"),
+        P(("pair", "side"), None, "head"),
         P(),
         P(),
-        P("head", "pool"),
+        P("head", ("pair", "side")),
     )
     return jax.shard_map(
-        on_device, mesh=mesh, in_specs=placed, out_specs=P(None, ("pool", "head")), check_vma=False
+        on_device, mesh=split, in_specs=placed, out_specs=P(None, ("pair", "side", "head")), check_vma=False
     )

time: 62.9 us -> 60.5 us (0.962)
  blocking collectives: 52.1 us -> 48.1 us
  starting transfers between devices: 0 us -> 2.04 us
    all_to_all x3, blocking collectives: 52.1 us -> 48.1 us  [the longest x1 20.2 us: on_device(): lax.all_to_all(packed.reshape(POOLS, CAP, LANES), ('pair', 'side'), split...]
    ppermute x0 -> x1, starting transfers between devices: none -> 2.04 us  [on_device(): weights = [out_weight, lax.ppermute(out_weight, 'side', [(0, 1), (1, 0)])]]
  transfers between devices with their start and end apart: 0 -> 1, of which waited for: 0 -> 0; matrix products, arithmetic and copies ran while one was open for 0% -> 0% of each run, Pallas kernels for 0% -> 12%
where the time goes in v3:
time: 60.5 us; the launch traced here: 60.3 us
  blocking collectives  48.1 us (80%)
  Pallas kernels  10.1 us (17%)
  starting transfers between devices  2.04 us (3%)
    all_to_all x1, blocking collectives, on_device(): lax.all_to_all(packed.reshape(POOLS, CAP, LANES), ('pair', 'side'), split...  20.2 us
    all_to_all x1, blocking collectives, on_device(): lax.all_to_all(partial, 'pair', split_axis=0, concat_axis=0, tiled=True)  14.1 us
    all_to_all x1, blocking collectives, on_device(): lax.all_to_all(projected, ('side', 'head'), split_axis=0, concat_axis=0,...  13.8 us
    pallas_call x1, Pallas kernels, score(): pl.pallas_call(holder_kernel, in_specs=[pl.BlockSpec(memory_space=pltpu.H...  7.08 us
    pallas_call x1, Pallas kernels, weigh(): pl.pallas_call(owner_kernel, in_specs=[pl.BlockSpec(memory_space=pltpu.VM...  2.15 us
    ppermute x1, starting transfers between devices, on_device(): weights = [out_weight, lax.ppermute(out_weight, 'side', [(0, 1), (1, 0)])]  2.04 us
  transfers between devices with their start and end apart: 1, of which 0 were waited for; matrix products, arithmetic and copies ran while one was open for 0% of the time, Pallas kernels for 12%

profile of v3, /device:TPU:1, one launch (start us, length us, event | category | flops | bytes accessed | tf_op | source)
XLA Modules:
  0.0 60.3 jit_solution(12501252365193622872)
XLA Ops:
  0.0 0.0 copy-start
  0.0 2.0 %collective-permute-start = (bf16[1024,256]{1,0:T(8,128)(2,1)}, bf16[1024,256]{1,0:T(8,128)(2,1)S(1)}, u32[]{:S(2)}, u32[]{:S(2)}) collective-permute-start(bf16[1024,256]{1,0:T(8,128)(2,1)} %refs_0_.1), channel_id=1, source_target_pairs={{0,8},{8,0},{1,9},{9,1},{2,10},{10,2},{3,11},{11,3},{4,12},{12,4},... | collective-permute-start | bytes 1572872 | tf_op jit(solution)/shard_map/ppermute | solution.py:397
  2.0 0.0 copy-start.1
  2.0 7.1 %score.1 = bf16[512,128]{1,0:T(8,128)(2,1)S(1)} custom-call(s32[8]{0:T(128)} %pos_hbm.1, bf16[8,1024]{1,0:T(8,128)(2,1)} %query_hbm.1, bf16[8,160,2048]{2,1,0:T(8,128)(2,1)} %bitcast.6, bf16[160,128]{1,0:T(8,128)(2,1)} %key_up_hbm.1, s32[8,1024]{1,0:T(8,128)} %chosen_hbm.1, s32[512,128]{1,0:T(8,128)} %bitcast.7, f32[184,128]{1,0:T(8,128)} %constant.4.clone.row_hbm, ...), custom_call_target="tpu_custom_call" | custom-call | tf_op jit(solution)/shard_map/score/pallas_call | solution.py:325
  9.1 20.2 %all_to_all.15 = bf16[32,16,128]{2,1,0:T(8,128)(2,1)S(1)} all-to-all(bf16[32,16,128]{2,1,0:T(8,128)(2,1)S(1)} %bitcast.5), channel_id=1, replica_groups=mesh['pair'=16,'side'=2,'head'=8] {'pair','side'}, dimensions={0} | all-to-all | bytes 262144 | tf_op jit(solution)/shard_map/all_to_all | solution.py:399
  29.3 0.0 collective-permute-done.refs_1_
  29.3 0.0 copy-done
  29.3 2.2 %weigh.1 = bf16[16,8,1024]{2,1,0:T(8,128)(2,1)S(1)} custom-call(bf16[512,128]{1,0:T(8,128)(2,1)S(1)} %bitcast.4, bf16[2048,8,128]{2,1,0:T(8,128)(2,1)S(1)} %copy-done), custom_call_target="tpu_custom_call" | custom-call | tf_op jit(solution)/shard_map/weigh/pallas_call | solution.py:354
  31.5 14.1 %all_to_all.16.gathered_ref = bf16[16,8,1024]{2,1,0:T(8,128)(2,1)S(1)} all-to-all(bf16[16,8,1024]{2,1,0:T(8,128)(2,1)S(1)} %weigh.1), channel_id=1, replica_groups=mesh['pair'=16,'side'=2,'head'=8] {'pair'}, dimensions={0} | all-to-all | bytes 524288 | tf_op jit(solution)/shard_map/all_to_all | solution.py:402
  45.6 0.0 copy-done.1
  45.6 0.3 combine.1
  45.9 13.8 %all_to_all.17.parts_ref = f32[16,8,128]{2,1,0:T(8,128)S(1)} all-to-all(f32[16,8,128]{2,1,0:T(8,128)S(1)} %combine.1), channel_id=1, replica_groups=mesh['pair'=16,'side'=2,'head'=8] {'side','head'}, dimensions={0} | all-to-all | bytes 131072 | tf_op jit(solution)/shard_map/all_to_all | solution.py:405
  59.7 0.6 finish.1
Async XLA Ops:
  0.0 29.3 %copy-start = (bf16[2048,8,128]{2,1,0:T(8,128)(2,1)S(1)}, bf16[2048,8,128]{2,1,0:T(8,128)(2,1)}, u32[]{:S(2)}) copy-start(bf16[2048,8,128]{2,1,0:T(8,128)(2,1)} %values_ref.1) | copy-start | bytes 12582916
  0.0 29.3 %collective-permute-start = (bf16[1024,256]{1,0:T(8,128)(2,1)}, bf16[1024,256]{1,0:T(8,128)(2,1)S(1)}, u32[]{:S(2)}, u32[]{:S(2)}) collective-permute-start(bf16[1024,256]{1,0:T(8,128)(2,1)} %refs_0_.1), channel_id=1, source_target_pairs={{0,8},{8,0},{1,9},{9,1},{2,10},{10,2},{3,11},{11,3},{4,12},{12,4},... | collective-permute-start | bytes 1572872 | tf_op jit(solution)/shard_map/ppermute | solution.py:397
  2.0 43.6 %copy-start.1 = (bf16[1024,256]{1,0:T(8,128)(2,1)S(1)}, bf16[1024,256]{1,0:T(8,128)(2,1)}, u32[]{:S(2)}) copy-start(bf16[1024,256]{1,0:T(8,128)(2,1)} %refs_0_.1) | copy-start | bytes 1572868

commit v4 on v3

--- a/solution.py
+++ b/solution.py
@@ -27,6 +27,7 @@
 SLOTS = 2048
 CHUNKS = SEQS * SPANS // LANES
 BIG_NEG = -1e30
+BATCH = 512
 
 f32 = jnp.float32
 bf16 = jnp.bfloat16
@@ -221,7 +222,7 @@
         copy.start()
     for copy in small:
         copy.wait()
-    pool = lax.axis_index("pair") * 2 + lax.axis_index("side")
+    pool = lax.axis_index("z") * 4 + lax.axis_index("xb") * 2 + lax.axis_index("side")
     plan(pool, chosen_ref, slot_ref, slot_scr, span_scr, seq_scr, meta_scr, mask_scr)
     rotate_queries(pos_ref, query_ref, row_ref, angle_scr, q_scr, q_out)
     key_angles(pool, column_ref, cos_scr, sin_scr)
@@ -260,11 +261,14 @@
     return levels
 
 
-def owner_kernel(packed_ref, values_ref, out_ref, slot_vec, slot_sca, sem, found_scr, sum_scr):
-    packed = packed_ref[...].astype(f32).T
-    slot_vec[...] = (packed[88:89] * 64.0 + packed[89:90]).astype(jnp.int32)
+def owner_kernel(packed_ref, values_ref, out_ref, slot_vec, slot_sca, sem, found_scr, left_scr, sum_scr):
+    rows = packed_ref[...]
+    pick = iota((8, LANES), 1)
+    slots = dot_nt(jnp.where(pick == 88, 64.0, jnp.where(pick == 89, 1.0, 0.0)).astype(bf16), rows)
+    slot_vec[...] = slots[:1].astype(jnp.int32)
     copy = pltpu.make_async_copy(slot_vec, slot_sca, sem)
     copy.start()
+    packed = dot_nt(onehot(iota((LANES, LANES), 0) == iota((LANES, LANES), 1)), rows)
     seq = packed[90:91]
     live = seq > 0.5
     mine = [seq == float(s + 1) for s in range(SEQS)]
@@ -279,17 +283,18 @@
         level_of = jnp.where(mine[s], top + jnp.log(total), level_of)
     factor = jnp.where(live, jnp.exp(level - level_of), 0.0)
     weights = [packed[t * HEADS : (t + 1) * HEADS] * factor for t in range(SPAN)]
+    left = [jnp.concatenate([jnp.where(mine[s], weights[t], 0.0) for s in range(SEQS)], axis=0).astype(bf16) for t in range(SPAN)]
+    left_scr[...] = jnp.concatenate(left, axis=1)
     copy.wait()
 
-    @pl.loop(0, ROWS // 16)
+    @pl.loop(0, ROWS // BATCH)
     def _(step):
-        for i in range(16):
-            row = step * 16 + i
+        for i in range(BATCH):
+            row = step * BATCH + i
             found_scr[pl.ds(pl.multiple_of(row * SPAN, SPAN), SPAN), :] = values_ref[slot_sca[0, row]].astype(f32)
 
-    left = [jnp.concatenate([jnp.where(mine[s], weights[t], 0.0) for s in range(SEQS)], axis=0).astype(bf16) for t in range(SPAN)]
     right = [found_scr[pl.ds(t, ROWS, stride=SPAN), :].astype(bf16) for t in range(SPAN)]
-    sum_scr[...] = dot(jnp.concatenate(left, axis=1), jnp.concatenate(right, axis=0))
+    sum_scr[...] = dot(left_scr[...], jnp.concatenate(right, axis=0))
     result = jnp.concatenate([sum_scr[pl.ds(h, SEQS, stride=HEADS), :] for h in range(HEADS)], axis=1).astype(bf16)
     for p in range(PAIRS):
         out_ref[p] = result
@@ -361,6 +366,7 @@
             pltpu.SMEM((1, ROWS), jnp.int32),
             pltpu.SemaphoreType.DMA,
             pltpu.VMEM((ROWS * SPAN, HD), f32),
+            pltpu.VMEM((SEQS * HEADS, ROWS * SPAN), bf16),
             pltpu.VMEM((SEQS * HEADS, HD), f32),
         ],
         compiler_params=pltpu.CompilerParams(vmem_limit_bytes=24 << 20),
@@ -396,10 +402,10 @@
     slot_rows = value_slot.reshape(-1, LANES)
     weights = [out_weight, lax.ppermute(out_weight, "side", [(0, 1), (1, 0)])]
     packed = score(query_pos, query, latent, key_up, chosen, slot_rows, row_table, column_table)
-    arrived = lax.all_to_all(packed.reshape(POOLS, CAP, LANES), ("pair", "side"), split_axis=0, concat_axis=0, tiled=True)
+    arrived = lax.all_to_all(packed.reshape(POOLS, CAP, LANES), ("z", "xb", "side"), split_axis=0, concat_axis=0, tiled=True)
     arrived, weights[1] = lax.optimization_barrier((arrived, weights[1]))
     partial = weigh(arrived.reshape(ROWS, LANES), value_cache)
-    gathered = lax.all_to_all(partial, "pair", split_axis=0, concat_axis=0, tiled=True)
+    gathered = lax.all_to_all(partial, ("xb", "z"), split_axis=0, concat_axis=0, tiled=True)
     groups = lax.axis_size("head")
     projected = combine(gathered, weights, groups)
     parts = lax.all_to_all(projected, ("side", "head"), split_axis=0, concat_axis=0, tiled=True)
@@ -407,17 +413,17 @@
 
 
 def solution(mesh):
-    split = Mesh(mesh.devices.reshape(PAIRS, 2, -1), ("pair", "side", "head"))
+    split = Mesh(mesh.devices.reshape(8, 2, 2, -1), ("z", "xb", "side", "head"))
     placed = (
         P(None, "head"),
         P(),
-        P(None, ("pair", "side"), None),
+        P(None, ("z", "xb", "side"), None),
         P(None, "head"),
-        P(("pair", "side"), None, "head"),
+        P(("z", "xb", "side"), None, "head"),
         P(),
         P(),
-        P("head", ("pair", "side")),
+        P("head", ("z", "xb", "side")),
     )
     return jax.shard_map(
-        on_device, mesh=split, in_specs=placed, out_specs=P(None, ("pair", "side", "head")), check_vma=False
+        on_device, mesh=split, in_specs=placed, out_specs=P(None, ("z", "xb", "side", "head")), check_vma=False
     )

time: 60.5 us -> 58.3 us (0.964)
  blocking collectives: 48.1 us -> 46.3 us
    all_to_all x2, blocking collectives: 34.3 us -> 32.4 us  [the longest x1 20.2 us: on_device(): lax.all_to_all(packed.reshape(POOLS, CAP, LANES), ('z', 'xb', 'side'), sp...]
where the time goes in v4:
time: 58.3 us; the launch traced here: 58.2 us
  blocking collectives  46.3 us (79%)
  Pallas kernels  9.82 us (17%)
  starting transfers between devices  2.04 us (3%)
    all_to_all x1, blocking collectives, on_device(): lax.all_to_all(packed.reshape(POOLS, CAP, LANES), ('z', 'xb', 'side'), sp...  20.2 us
    all_to_all x1, blocking collectives, on_device(): lax.all_to_all(projected, ('side', 'head'), split_axis=0, concat_axis=0,...  13.8 us
    all_to_all x1, blocking collectives, on_device(): lax.all_to_all(partial, ('xb', 'z'), split_axis=0, concat_axis=0, tiled=T...  12.3 us
    pallas_call x1, Pallas kernels, score(): pl.pallas_call(holder_kernel, in_specs=[pl.BlockSpec(memory_space=pltpu.H...  7.08 us
    ppermute x1, starting transfers between devices, on_device(): weights = [out_weight, lax.ppermute(out_weight, 'side', [(0, 1), (1, 0)])]  2.04 us
    pallas_call x1, Pallas kernels, weigh(): pl.pallas_call(owner_kernel, in_specs=[pl.BlockSpec(memory_space=pltpu.VM...  1.84 us
  transfers between devices with their start and end apart: 1, of which 0 were waited for; matrix products, arithmetic and copies ran while one was open for 0% of the time, Pallas kernels for 12%

profile of v4, /device:TPU:1, one launch (start us, length us, event | category | flops | bytes accessed | tf_op | source)
XLA Modules:
  0.0 58.2 jit_solution(16317863563094207895)
XLA Ops:
  0.0 0.0 copy-start
  0.0 2.0 %collective-permute-start = (bf16[1024,256]{1,0:T(8,128)(2,1)}, bf16[1024,256]{1,0:T(8,128)(2,1)S(1)}, u32[]{:S(2)}, u32[]{:S(2)}) collective-permute-start(bf16[1024,256]{1,0:T(8,128)(2,1)} %refs_0_.1), channel_id=1, source_target_pairs={{0,8},{8,0},{1,9},{9,1},{2,10},{10,2},{3,11},{11,3},{4,12},{12,4},... | collective-permute-start | bytes 1572872 | tf_op jit(solution)/shard_map/ppermute | solution.py:403
  2.0 0.0 copy-start.1
  2.0 7.1 %score.1 = bf16[512,128]{1,0:T(8,128)(2,1)S(1)} custom-call(s32[8]{0:T(128)} %pos_hbm.1, bf16[8,1024]{1,0:T(8,128)(2,1)} %query_hbm.1, bf16[8,160,2048]{2,1,0:T(8,128)(2,1)} %bitcast.6, bf16[160,128]{1,0:T(8,128)(2,1)} %key_up_hbm.1, s32[8,1024]{1,0:T(8,128)} %chosen_hbm.1, s32[512,128]{1,0:T(8,128)} %bitcast.7, f32[184,128]{1,0:T(8,128)} %constant.4.clone.row_hbm, ...), custom_call_target="tpu_custom_call" | custom-call | tf_op jit(solution)/shard_map/score/pallas_call | solution.py:330
  9.1 20.2 %all_to_all.15 = bf16[32,16,128]{2,1,0:T(8,128)(2,1)S(1)} all-to-all(bf16[32,16,128]{2,1,0:T(8,128)(2,1)S(1)} %bitcast.5), channel_id=1, replica_groups=mesh['z'=8,'xb'=2,'side'=2,'head'=8] {'z','xb','side'}, dimensions={0} | all-to-all | bytes 262144 | tf_op jit(solution)/shard_map/all_to_all | solution.py:405
  29.3 0.0 collective-permute-done.refs_1_
  29.3 0.0 copy-done
  29.3 1.8 %weigh.1 = bf16[16,8,1024]{2,1,0:T(8,128)(2,1)S(1)} custom-call(bf16[512,128]{1,0:T(8,128)(2,1)S(1)} %bitcast.4, bf16[2048,8,128]{2,1,0:T(8,128)(2,1)S(1)} %copy-done), custom_call_target="tpu_custom_call" | custom-call | tf_op jit(solution)/shard_map/weigh/pallas_call | solution.py:359
  31.2 12.3 %all_to_all.16.gathered_ref = bf16[16,8,1024]{2,1,0:T(8,128)(2,1)S(1)} all-to-all(bf16[16,8,1024]{2,1,0:T(8,128)(2,1)S(1)} %weigh.1), channel_id=1, replica_groups=mesh['z'=8,'xb'=2,'side'=2,'head'=8] {'xb','z'}, dimensions={0} | all-to-all | bytes 524288 | tf_op jit(solution)/shard_map/all_to_all | solution.py:408
  43.4 0.0 copy-done.1
  43.4 0.3 combine.1
  43.7 13.8 %all_to_all.17.parts_ref = f32[16,8,128]{2,1,0:T(8,128)S(1)} all-to-all(f32[16,8,128]{2,1,0:T(8,128)S(1)} %combine.1), channel_id=1, replica_groups=mesh['z'=8,'xb'=2,'side'=2,'head'=8] {'side','head'}, dimensions={0} | all-to-all | bytes 131072 | tf_op jit(solution)/shard_map/all_to_all | solution.py:411
  57.6 0.6 %finish.1 = bf16[8,32]{1,0:T(8,128)(2,1)} custom-call(f32[16,8,128]{2,1,0:T(8,128)S(1)} %all_to_all.17.parts_ref), custom_call_target="tpu_custom_call" | custom-call | tf_op jit(solution)/shard_map/finish/pallas_call | solution.py:389
Async XLA Ops:
  0.0 29.3 %copy-start = (bf16[2048,8,128]{2,1,0:T(8,128)(2,1)S(1)}, bf16[2048,8,128]{2,1,0:T(8,128)(2,1)}, u32[]{:S(2)}) copy-start(bf16[2048,8,128]{2,1,0:T(8,128)(2,1)} %values_ref.1) | copy-start | bytes 12582916
  0.0 29.3 %collective-permute-start = (bf16[1024,256]{1,0:T(8,128)(2,1)}, bf16[1024,256]{1,0:T(8,128)(2,1)S(1)}, u32[]{:S(2)}, u32[]{:S(2)}) collective-permute-start(bf16[1024,256]{1,0:T(8,128)(2,1)} %refs_0_.1), channel_id=1, source_target_pairs={{0,8},{8,0},{1,9},{9,1},{2,10},{10,2},{3,11},{11,3},{4,12},{12,4},... | collective-permute-start | bytes 1572872 | tf_op jit(solution)/shard_map/ppermute | solution.py:403
  2.0 41.4 %copy-start.1 = (bf16[1024,256]{1,0:T(8,128)(2,1)S(1)}, bf16[1024,256]{1,0:T(8,128)(2,1)}, u32[]{:S(2)}) copy-start(bf16[1024,256]{1,0:T(8,128)(2,1)} %refs_0_.1) | copy-start | bytes 1572868

commit v5 on v4

--- a/solution.py
+++ b/solution.py
@@ -106,7 +106,7 @@
         sin_scr[:, c * LANES : (c + 1) * LANES] = sa * c3 + ca * s3
 
 
-def plan(pool, chosen_ref, slot_ref, slot_scr, span_scr, seq_scr, meta_scr, mask_scr):
+def plan(rest, pool, chosen_ref, slot_ref, slot_scr, span_scr, seq_scr, meta_scr, mask_scr):
     relative = chosen_ref[...] - pool * SPANS
     here = (relative >= 0) & (relative < SPANS)
     row_code = jnp.where(here, 2 * iota(relative.shape, 0) + (relative >> 7), -1)
@@ -116,6 +116,8 @@
     right = [onehot(iota((LANES, picks), 0) == lane_code[s : s + 1, :]) for s in range(SEQS)]
     member = dot_nt(jnp.concatenate(left, axis=1), jnp.concatenate(right, axis=1))
     mask_scr[...] = dot(member.astype(bf16), onehot(iota((LANES, LANES * SPAN), 0) == (iota((LANES, LANES * SPAN), 1) >> 3)))
+    for copy in rest:
+        copy.wait()
     for s in range(SEQS):
         slot_scr[2 * s : 2 * s + 2, :] = slot_ref[pl.ds(s * (SPANS * POOLS // LANES) + 2 * pool, 2), :]
     slots = slot_scr[...]
@@ -220,10 +222,9 @@
     latents = [pltpu.make_async_copy(latent_hbm.at[s], latent_ref.at[s], sems.at[len(small) + s]) for s in range(SEQS)]
     for copy in latents:
         copy.start()
-    for copy in small:
-        copy.wait()
+    small[0].wait()
     pool = lax.axis_index("z") * 4 + lax.axis_index("xb") * 2 + lax.axis_index("side")
-    plan(pool, chosen_ref, slot_ref, slot_scr, span_scr, seq_scr, meta_scr, mask_scr)
+    plan(small[1:], pool, chosen_ref, slot_ref, slot_scr, span_scr, seq_scr, meta_scr, mask_scr)
     rotate_queries(pos_ref, query_ref, row_ref, angle_scr, q_scr, q_out)
     key_angles(pool, column_ref, cos_scr, sin_scr)
     up_scr[...] = key_up_ref[...].astype(f32).T.astype(bf16)

time: 58.3 us -> 58.2 us (level)
  no operation moved by 1% of the time
where the time goes in v5:
time: 58.2 us; the launch traced here: 58 us
  blocking collectives  46.3 us (80%)
  Pallas kernels  9.66 us (17%)
  starting transfers between devices  2.04 us (4%)
    all_to_all x1, blocking collectives, on_device(): lax.all_to_all(packed.reshape(POOLS, CAP, LANES), ('z', 'xb', 'side'), sp...  20.2 us
    all_to_all x1, blocking collectives, on_device(): lax.all_to_all(projected, ('side', 'head'), split_axis=0, concat_axis=0,...  13.8 us
    all_to_all x1, blocking collectives, on_device(): lax.all_to_all(partial, ('xb', 'z'), split_axis=0, concat_axis=0, tiled=T...  12.3 us
    pallas_call x1, Pallas kernels, score(): pl.pallas_call(holder_kernel, in_specs=[pl.BlockSpec(memory_space=pltpu.H...  6.92 us
    ppermute x1, starting transfers between devices, on_device(): weights = [out_weight, lax.ppermute(out_weight, 'side', [(0, 1), (1, 0)])]  2.04 us
    pallas_call x1, Pallas kernels, weigh(): pl.pallas_call(owner_kernel, in_specs=[pl.BlockSpec(memory_space=pltpu.VM...  1.85 us
  transfers between devices with their start and end apart: 1, of which 0 were waited for; matrix products, arithmetic and copies ran while one was open for 0% of the time, Pallas kernels for 12%

profile of v5, /device:TPU:1, one launch (start us, length us, event | category | flops | bytes accessed | tf_op | source)
XLA Modules:
  0.0 58.0 jit_solution(10956811700402073292)
XLA Ops:
  0.0 0.0 copy-start
  0.0 2.0 %collective-permute-start = (bf16[1024,256]{1,0:T(8,128)(2,1)}, bf16[1024,256]{1,0:T(8,128)(2,1)S(1)}, u32[]{:S(2)}, u32[]{:S(2)}) collective-permute-start(bf16[1024,256]{1,0:T(8,128)(2,1)} %refs_0_.1), channel_id=1, source_target_pairs={{0,8},{8,0},{1,9},{9,1},{2,10},{10,2},{3,11},{11,3},{4,12},{12,4},... | collective-permute-start | bytes 1572872 | tf_op jit(solution)/shard_map/ppermute | solution.py:404
  2.0 0.0 copy-start.1
  2.0 6.9 %score.1 = bf16[512,128]{1,0:T(8,128)(2,1)S(1)} custom-call(s32[8]{0:T(128)} %pos_hbm.1, bf16[8,1024]{1,0:T(8,128)(2,1)} %query_hbm.1, bf16[8,160,2048]{2,1,0:T(8,128)(2,1)} %bitcast.6, bf16[160,128]{1,0:T(8,128)(2,1)} %key_up_hbm.1, s32[8,1024]{1,0:T(8,128)} %chosen_hbm.1, s32[512,128]{1,0:T(8,128)} %bitcast.7, f32[184,128]{1,0:T(8,128)} %constant.4.clone.row_hbm, ...), custom_call_target="tpu_custom_call" | custom-call | tf_op jit(solution)/shard_map/score/pallas_call | solution.py:331
  9.0 20.2 %all_to_all.15 = bf16[32,16,128]{2,1,0:T(8,128)(2,1)S(1)} all-to-all(bf16[32,16,128]{2,1,0:T(8,128)(2,1)S(1)} %bitcast.5), channel_id=1, replica_groups=mesh['z'=8,'xb'=2,'side'=2,'head'=8] {'z','xb','side'}, dimensions={0} | all-to-all | bytes 262144 | tf_op jit(solution)/shard_map/all_to_all | solution.py:406
  29.1 0.0 collective-permute-done.refs_1_
  29.1 0.0 copy-done
  29.1 1.8 %weigh.1 = bf16[16,8,1024]{2,1,0:T(8,128)(2,1)S(1)} custom-call(bf16[512,128]{1,0:T(8,128)(2,1)S(1)} %bitcast.4, bf16[2048,8,128]{2,1,0:T(8,128)(2,1)S(1)} %copy-done), custom_call_target="tpu_custom_call" | custom-call | tf_op jit(solution)/shard_map/weigh/pallas_call | solution.py:360
  31.0 12.3 %all_to_all.16.gathered_ref = bf16[16,8,1024]{2,1,0:T(8,128)(2,1)S(1)} all-to-all(bf16[16,8,1024]{2,1,0:T(8,128)(2,1)S(1)} %weigh.1), channel_id=1, replica_groups=mesh['z'=8,'xb'=2,'side'=2,'head'=8] {'xb','z'}, dimensions={0} | all-to-all | bytes 524288 | tf_op jit(solution)/shard_map/all_to_all | solution.py:409
  43.3 0.0 copy-done.1
  43.3 0.3 combine.1
  43.6 13.8 %all_to_all.17.parts_ref = f32[16,8,128]{2,1,0:T(8,128)S(1)} all-to-all(f32[16,8,128]{2,1,0:T(8,128)S(1)} %combine.1), channel_id=1, replica_groups=mesh['z'=8,'xb'=2,'side'=2,'head'=8] {'side','head'}, dimensions={0} | all-to-all | bytes 131072 | tf_op jit(solution)/shard_map/all_to_all | solution.py:412
  57.4 0.6 %finish.1 = bf16[8,32]{1,0:T(8,128)(2,1)} custom-call(f32[16,8,128]{2,1,0:T(8,128)S(1)} %all_to_all.17.parts_ref), custom_call_target="tpu_custom_call" | custom-call | tf_op jit(solution)/shard_map/finish/pallas_call | solution.py:390
Async XLA Ops:
  0.0 29.1 %copy-start = (bf16[2048,8,128]{2,1,0:T(8,128)(2,1)S(1)}, bf16[2048,8,128]{2,1,0:T(8,128)(2,1)}, u32[]{:S(2)}) copy-start(bf16[2048,8,128]{2,1,0:T(8,128)(2,1)} %values_ref.1) | copy-start | bytes 12582916
  0.0 29.1 %collective-permute-start = (bf16[1024,256]{1,0:T(8,128)(2,1)}, bf16[1024,256]{1,0:T(8,128)(2,1)S(1)}, u32[]{:S(2)}, u32[]{:S(2)}) collective-permute-start(bf16[1024,256]{1,0:T(8,128)(2,1)} %refs_0_.1), channel_id=1, source_target_pairs={{0,8},{8,0},{1,9},{9,1},{2,10},{10,2},{3,11},{11,3},{4,12},{12,4},... | collective-permute-start | bytes 1572872 | tf_op jit(solution)/shard_map/ppermute | solution.py:404
  2.0 41.2 %copy-start.1 = (bf16[1024,256]{1,0:T(8,128)(2,1)S(1)}, bf16[1024,256]{1,0:T(8,128)(2,1)}, u32[]{:S(2)}) copy-start(bf16[1024,256]{1,0:T(8,128)(2,1)} %refs_0_.1) | copy-start | bytes 1572868

commit v6 on v5

--- a/solution.py
+++ b/solution.py
@@ -121,7 +121,8 @@
     for s in range(SEQS):
         slot_scr[2 * s : 2 * s + 2, :] = slot_ref[pl.ds(s * (SPANS * POOLS // LANES) + 2 * pool, 2), :]
     slots = slot_scr[...]
-    owner = jnp.where(member > 0.5, slots >> 11, -1)
+    owner = slots >> 11
+    owner = jnp.where(member > 0.5, (owner & 3) * 8 + (owner >> 2), -1)
     local_slot = slots & (SLOTS - 1)
     owners = [jnp.where(iota((POOLS, LANES), 0) == owner[c : c + 1, :], 1.0, 0.0) for c in range(CHUNKS)]
     earlier = iota((LANES, 2 * LANES), 0) < iota((LANES, 2 * LANES), 1)
@@ -403,7 +404,7 @@
     slot_rows = value_slot.reshape(-1, LANES)
     weights = [out_weight, lax.ppermute(out_weight, "side", [(0, 1), (1, 0)])]
     packed = score(query_pos, query, latent, key_up, chosen, slot_rows, row_table, column_table)
-    arrived = lax.all_to_all(packed.reshape(POOLS, CAP, LANES), ("z", "xb", "side"), split_axis=0, concat_axis=0, tiled=True)
+    arrived = lax.all_to_all(packed.reshape(POOLS, CAP, LANES), ("xb", "side", "z"), split_axis=0, concat_axis=0, tiled=True)
     arrived, weights[1] = lax.optimization_barrier((arrived, weights[1]))
     partial = weigh(arrived.reshape(ROWS, LANES), value_cache)
     gathered = lax.all_to_all(partial, ("xb", "z"), split_axis=0, concat_axis=0, tiled=True)

time: 58.2 us -> 58.2 us (level)
  no operation moved by 1% of the time
where the time goes in v6:
time: 58.2 us; the launch traced here: 58 us
  blocking collectives  46.3 us (80%)
  Pallas kernels  9.65 us (17%)
  starting transfers between devices  2.04 us (4%)
    all_to_all x1, blocking collectives, on_device(): lax.all_to_all(packed.reshape(POOLS, CAP, LANES), ('xb', 'side', 'z'), sp...  20 us
    all_to_all x1, blocking collectives, on_device(): lax.all_to_all(projected, ('side', 'head'), split_axis=0, concat_axis=0,...  13.8 us
    all_to_all x1, blocking collectives, on_device(): lax.all_to_all(partial, ('xb', 'z'), split_axis=0, concat_axis=0, tiled=T...  12.5 us
    pallas_call x1, Pallas kernels, score(): pl.pallas_call(holder_kernel, in_specs=[pl.BlockSpec(memory_space=pltpu.H...  6.91 us
    ppermute x1, starting transfers between devices, on_device(): weights = [out_weight, lax.ppermute(out_weight, 'side', [(0, 1), (1, 0)])]  2.04 us
    pallas_call x1, Pallas kernels, weigh(): pl.pallas_call(owner_kernel, in_specs=[pl.BlockSpec(memory_space=pltpu.VM...  1.85 us
  transfers between devices with their start and end apart: 1, of which 0 were waited for; matrix products, arithmetic and copies ran while one was open for 0% of the time, Pallas kernels for 12%

profile of v6, /device:TPU:1, one launch (start us, length us, event | category | flops | bytes accessed | tf_op | source)
XLA Modules:
  0.0 58.0 jit_solution(7380809062047999681)
XLA Ops:
  0.0 0.0 copy-start
  0.0 2.0 %collective-permute-start = (bf16[1024,256]{1,0:T(8,128)(2,1)}, bf16[1024,256]{1,0:T(8,128)(2,1)S(1)}, u32[]{:S(2)}, u32[]{:S(2)}) collective-permute-start(bf16[1024,256]{1,0:T(8,128)(2,1)} %refs_0_.1), channel_id=1, source_target_pairs={{0,8},{8,0},{1,9},{9,1},{2,10},{10,2},{3,11},{11,3},{4,12},{12,4},... | collective-permute-start | bytes 1572872 | tf_op jit(solution)/shard_map/ppermute | solution.py:405
  2.0 0.0 copy-start.1
  2.0 6.9 %score.1 = bf16[512,128]{1,0:T(8,128)(2,1)S(1)} custom-call(s32[8]{0:T(128)} %pos_hbm.1, bf16[8,1024]{1,0:T(8,128)(2,1)} %query_hbm.1, bf16[8,160,2048]{2,1,0:T(8,128)(2,1)} %bitcast.6, bf16[160,128]{1,0:T(8,128)(2,1)} %key_up_hbm.1, s32[8,1024]{1,0:T(8,128)} %chosen_hbm.1, s32[512,128]{1,0:T(8,128)} %bitcast.7, f32[184,128]{1,0:T(8,128)} %constant.4.clone.row_hbm, ...), custom_call_target="tpu_custom_call" | custom-call | tf_op jit(solution)/shard_map/score/pallas_call | solution.py:332
  9.0 20.0 %all_to_all.15 = bf16[32,16,128]{2,1,0:T(8,128)(2,1)S(1)} all-to-all(bf16[32,16,128]{2,1,0:T(8,128)(2,1)S(1)} %bitcast.5), channel_id=1, replica_groups=mesh['z'=8,'xb'=2,'side'=2,'head'=8] {'xb','side','z'}, dimensions={0} | all-to-all | bytes 262144 | tf_op jit(solution)/shard_map/all_to_all | solution.py:407
  28.9 0.0 collective-permute-done.refs_1_
  28.9 0.0 copy-done
  28.9 1.8 %weigh.1 = bf16[16,8,1024]{2,1,0:T(8,128)(2,1)S(1)} custom-call(bf16[512,128]{1,0:T(8,128)(2,1)S(1)} %bitcast.4, bf16[2048,8,128]{2,1,0:T(8,128)(2,1)S(1)} %copy-done), custom_call_target="tpu_custom_call" | custom-call | tf_op jit(solution)/shard_map/weigh/pallas_call | solution.py:361
  30.8 12.5 %all_to_all.16.gathered_ref = bf16[16,8,1024]{2,1,0:T(8,128)(2,1)S(1)} all-to-all(bf16[16,8,1024]{2,1,0:T(8,128)(2,1)S(1)} %weigh.1), channel_id=1, replica_groups=mesh['z'=8,'xb'=2,'side'=2,'head'=8] {'xb','z'}, dimensions={0} | all-to-all | bytes 524288 | tf_op jit(solution)/shard_map/all_to_all | solution.py:410
  43.3 0.0 copy-done.1
  43.3 0.3 combine.1
  43.6 13.8 %all_to_all.17.parts_ref = f32[16,8,128]{2,1,0:T(8,128)S(1)} all-to-all(f32[16,8,128]{2,1,0:T(8,128)S(1)} %combine.1), channel_id=1, replica_groups=mesh['z'=8,'xb'=2,'side'=2,'head'=8] {'side','head'}, dimensions={0} | all-to-all | bytes 131072 | tf_op jit(solution)/shard_map/all_to_all | solution.py:413
  57.4 0.6 %finish.1 = bf16[8,32]{1,0:T(8,128)(2,1)} custom-call(f32[16,8,128]{2,1,0:T(8,128)S(1)} %all_to_all.17.parts_ref), custom_call_target="tpu_custom_call" | custom-call | tf_op jit(solution)/shard_map/finish/pallas_call | solution.py:391
Async XLA Ops:
  0.0 28.9 %copy-start = (bf16[2048,8,128]{2,1,0:T(8,128)(2,1)S(1)}, bf16[2048,8,128]{2,1,0:T(8,128)(2,1)}, u32[]{:S(2)}) copy-start(bf16[2048,8,128]{2,1,0:T(8,128)(2,1)} %values_ref.1) | copy-start | bytes 12582916
  0.0 28.9 %collective-permute-start = (bf16[1024,256]{1,0:T(8,128)(2,1)}, bf16[1024,256]{1,0:T(8,128)(2,1)S(1)}, u32[]{:S(2)}, u32[]{:S(2)}) collective-permute-start(bf16[1024,256]{1,0:T(8,128)(2,1)} %refs_0_.1), channel_id=1, source_target_pairs={{0,8},{8,0},{1,9},{9,1},{2,10},{10,2},{3,11},{11,3},{4,12},{12,4},... | collective-permute-start | bytes 1572872 | tf_op jit(solution)/shard_map/ppermute | solution.py:405
  2.0 41.3 %copy-start.1 = (bf16[1024,256]{1,0:T(8,128)(2,1)S(1)}, bf16[1024,256]{1,0:T(8,128)(2,1)}, u32[]{:S(2)}) copy-start(bf16[1024,256]{1,0:T(8,128)(2,1)} %refs_0_.1) | copy-start | bytes 1572868
